TPU v7x, 32 devices: a whole 2x2x4 slice. The times are simulated.
32 devices in a mesh: seq: 8 (over z, x), head: 4 (over y, core).
Axes of the slice: x: 2, y: 2, z: 4, core: 2. Of those that a mesh axis runs over, the one named last changes fastest.
Arguments:
- tokens: bfloat16 [4096, 4096], P(('seq', 'head')), may hold values from -6 to 6
- in_weight: bfloat16 [4096, 8192], P('seq', 'head'), may hold values from -0.09375 to 0.09375
- write_proj: bfloat16 [4096, 128], P(('seq', 'head')), may hold values from -6 to 6
- read_proj: bfloat16 [4096, 128], P(('seq', 'head')), may hold values from -0.5 to 0.5
- log_decay: float32 [128, 4096], P('head', 'seq'), may hold values from -1.1 to 0, as said below
- level_gain: float32 [7, 128, 4096], P(None, 'head', 'seq'), may hold values from 0 to 1, as said below
- out_grad: bfloat16 [4096, 8192], P('seq', 'head'), may hold values from -6 to 6
Outputs:
- layer_out: bfloat16 [4096, 8192], P('seq', 'head')
- weight_grad: bfloat16 [4096, 8192], P('seq', 'head')
Inputs may be any that keep to these rules, and one draw needn't show every extreme that they name: `log_decay`: Log-decays are non-positive. `level_gain`: level weights are positive.
All inputs are finite; a program needn't handle non-finite values.
Results may differ from a plain program's by a relative error of at most 0.02.
Values may be sent and summed in bfloat16 or wider, within the bound.
A program may use at most 128 MiB of HBM per device.

v0:
```python
import jax
import jax.numpy as jnp
from jax import lax
from jax.sharding import PartitionSpec as P

HEAD_DIM = 64
STATE = 128
CH = 64


def swapped(value, axis, apart):
    mask = 2**apart
    pairs = [(source, source ^ mask) for source in range(lax.axis_size(axis))]
    return lax.ppermute(value, axis, pairs)


def stretch_levels(length, level_count):
    stretches = jnp.arange(length, dtype=jnp.int32) // CH
    level_table = jnp.zeros((length, length), jnp.int32)
    for offset in range(level_count - 1):
        level_table = level_table + (
            stretches[:, None] >> offset != stretches[None, :] >> offset
        ).astype(jnp.int32)
    return level_table


def head_terms(scores, level_table, causal, cumulative, gain_rows, values, grad_rows):
    gain_table = jnp.zeros(scores.shape, jnp.float32)
    for number in range(gain_rows.shape[0]):
        gain_table = gain_table + jnp.where(level_table == number, gain_rows[number][:, None], 0.0)
    differ = cumulative[:, None] - cumulative[None, :]
    decays = jnp.where(causal, jnp.exp(jnp.where(causal, differ, 0.0)), 0.0)
    weights = (gain_table * decays * scores).astype(jnp.bfloat16)
    forward = jnp.dot(weights, values, preferred_element_type=jnp.float32)
    backward = lax.dot_general(
        weights, grad_rows, (((0,), (0,)), ((), ())), preferred_element_type=jnp.float32
    )
    return (forward, backward)


def merge_pending(pending, partner_pending, bit_level, is_upper, own_decay, partner_decay):
    rest_levels = pending[bit_level + 1 :]
    partner_rest = partner_pending[1:]
    merged = jnp.where(
        is_upper,
        partner_rest + partner_decay[None, :, None, None] * rest_levels,
        rest_levels + own_decay[None, :, None, None] * partner_rest,
    )
    return pending.at[bit_level + 1 :].set(merged)


def per_device(tokens, in_weight, write_proj, read_proj, log_decay, level_gain, out_grad):
    full_tokens, write_rows, read_rows = (
        lax.all_gather(tokens, "head", axis=0, tiled=True),
        lax.all_gather(write_proj, "head", axis=0, tiled=True),
        lax.all_gather(read_proj, "head", axis=0, tiled=True),
    )
    tok_len = full_tokens.shape[0]
    head_count = log_decay.shape[0]
    columns = in_weight.shape[1]
    local_count = (tok_len // CH).bit_length()
    seq_count = lax.axis_size("seq").bit_length() - 1
    token_position = lax.axis_index("seq")
    tok_part = full_tokens
    projected = jnp.dot(
        tok_part,
        lax.all_gather(in_weight, "seq", axis=0, tiled=True),
        preferred_element_type=jnp.float32,
    )
    values = projected.astype(jnp.bfloat16).reshape(tok_len, head_count, HEAD_DIM)
    grad_rows = out_grad.reshape(tok_len, head_count, HEAD_DIM)
    cumulative = jnp.cumsum(log_decay, axis=1)
    totals = cumulative[:, -1]
    key_rows = (
        jnp.exp(totals[:, None] - cumulative)[:, :, None] * write_rows.astype(jnp.float32)[None]
    ).astype(jnp.bfloat16)
    seg_state = jnp.einsum("htn,thp->hnp", key_rows, values, preferred_element_type=jnp.float32)
    query_scale = level_gain[local_count:].transpose(1, 2, 0) * jnp.exp(cumulative)[:, :, None]
    flat_query = (
        (query_scale[..., None] * read_rows.astype(jnp.float32)[None, :, None, :])
        .astype(jnp.bfloat16)
        .reshape(head_count, tok_len, seq_count * STATE)
    )
    level_grads = jnp.einsum(
        "htk,thp->hkp", flat_query, grad_rows, preferred_element_type=jnp.float32
    )
    level_grads = level_grads.reshape(head_count, seq_count, STATE, HEAD_DIM).transpose(1, 0, 2, 3)
    scores = lax.dot_general(
        read_rows, write_rows, (((1,), (1,)), ((), ())), preferred_element_type=jnp.float32
    )
    level_table = stretch_levels(tok_len, local_count)
    steps_idx = jnp.arange(tok_len, dtype=jnp.int32)
    causal = steps_idx[:, None] >= steps_idx[None, :]
    local_gain = level_gain[:local_count]

    def one_head(number):
        cum_head = cumulative[number]
        gain_head = lax.dynamic_index_in_dim(local_gain, number, 1, keepdims=False)
        value_head = lax.dynamic_index_in_dim(values, number, 1, keepdims=False)
        grad_head = lax.dynamic_index_in_dim(grad_rows, number, 1, keepdims=False)
        return head_terms(scores, level_table, causal, cum_head, gain_head, value_head, grad_head)

    local_out, local_grad = lax.map(one_head, jnp.arange(head_count))
    bit_flags = [token_position >> bit_level & 1 == 1 for bit_level in range(seq_count)]
    bit_mask = jnp.stack([flag.astype(jnp.float32) for flag in bit_flags])
    prefix = jnp.ones_like(totals)
    block_decay = jnp.exp(totals)
    block_state = seg_state
    buckets = []
    pending = level_grads * bit_mask[:, None, None, None]
    suffix = jnp.ones_like(totals)
    state_grad = jnp.zeros_like(seg_state)
    saved_decays = []
    for bit_level in range(seq_count):
        partner_decay, partner_state = (
            swapped(block_decay.astype(jnp.bfloat16), "seq", bit_level).astype(block_decay.dtype),
            swapped(block_state.astype(jnp.bfloat16), "seq", bit_level).astype(block_state.dtype),
        )
        is_upper = bit_flags[bit_level]
        buckets.append(jnp.where(is_upper, prefix[:, None, None] * partner_state, 0.0))
        saved_decays.append((block_decay, partner_decay))
        block_state = jnp.where(
            is_upper,
            block_decay[:, None, None] * partner_state + block_state,
            partner_decay[:, None, None] * block_state + partner_state,
        )
        prefix = jnp.where(is_upper, partner_decay * prefix, prefix)
        block_decay = partner_decay * block_decay
    for bit_level in range(seq_count):
        own_decay, partner_decay = saved_decays[bit_level]
        partner_pending = swapped(
            pending[bit_level:].astype(jnp.bfloat16), "seq", bit_level
        ).astype(jnp.float32)
        is_upper = bit_flags[bit_level]
        state_grad = state_grad + jnp.where(
            is_upper, 0.0, suffix[:, None, None] * partner_pending[0]
        )
        pending = merge_pending(
            pending, partner_pending, bit_level, is_upper, own_decay, partner_decay
        )
        suffix = jnp.where(is_upper, suffix, suffix * partner_decay)
    bucket_half = (
        jnp.stack(buckets)
        .transpose(1, 0, 2, 3)
        .reshape(head_count, seq_count * STATE, HEAD_DIM)
        .astype(jnp.bfloat16)
    )
    cross_term = jnp.einsum(
        "htk,hkp->thp", flat_query, bucket_half, preferred_element_type=jnp.float32
    )
    layer_out = (
        (cross_term + local_out.transpose(1, 0, 2)).astype(jnp.bfloat16).reshape(tok_len, columns)
    )
    state_half = state_grad.astype(jnp.bfloat16)
    cross_grad = jnp.einsum(
        "htn,hnp->thp", key_rows, state_half, preferred_element_type=jnp.float32
    )
    values_grad = (
        (cross_grad + local_grad.transpose(1, 0, 2)).astype(jnp.bfloat16).reshape(tok_len, columns)
    )
    tok_part = full_tokens
    weight_grad = lax.psum_scatter(
        lax.dot_general(
            tok_part, values_grad, (((0,), (0,)), ((), ())), preferred_element_type=jnp.float32
        ).astype(jnp.bfloat16),
        "seq",
        scatter_dimension=0,
        tiled=True,
    )
    return (layer_out, weight_grad)


def solution(mesh):
    in_specs = (
        P(("seq", "head"), None),
        P("seq", "head"),
        P(("seq", "head"), None),
        P(("seq", "head"), None),
        P("head", "seq"),
        P(None, "head", "seq"),
        P("seq", "head"),
    )
    out_specs = (P("seq", "head"), P("seq", "head"))
    return jax.shard_map(
        per_device, mesh=mesh, in_specs=in_specs, out_specs=out_specs, check_vma=False
    )
```

profile of v0, /device:TPU:0, one launch (start us, length us, event | category | flops | bytes accessed | tf_op | source)
XLA Modules:
  0.0 997.6 jit_solution(1269961244496982938)
XLA Ops:
  11.7 6.5 all_gather.15
  20.9 8.3 fusion.22
  29.3 9.1 convolution_bitcast_fusion.2
  41.2 50.5 %collective-permute-done.1 = bf16[32]{0:T(256)(128)(2,1)S(1)} collective-permute-done((bf16[32]{0:T(256)(128)(2,1)S(1)}, bf16[32]{0:T(256)(128)(2,1)S(1)}, u32[]{:S(2)}, u32[]{:S(2)}) %collective-permute-start.1) | collective-permute-done | bytes 96 | tf_op jit(solution)/shard_map/ppermute | solution.py:14
  97.6 5.6 all_gather.12
  105.7 47.9 %collective-permute-done.3 = bf16[32]{0:T(256)(128)(2,1)S(1)} collective-permute-done((bf16[32]{0:T(256)(128)(2,1)S(1)}, bf16[32]{0:T(256)(128)(2,1)S(1)}, u32[]{:S(2)}, u32[]{:S(2)}) %collective-permute-start.3) | collective-permute-done | bytes 96 | tf_op jit(solution)/shard_map/ppermute | solution.py:14
  157.5 160.9 %all-gather.5.cloned.1.call-done = bf16[4096,2048]{1,0:T(8,128)(2,1)} async-done(((bf16[512,2048]{1,0:T(8,128)(2,1)}), bf16[4096,2048]{1,0:T(8,128)(2,1)}) %all-gather.5.cloned.1.call-update) | async-done | bytes 16777232 | tf_op jit(solution)/shard_map/all_gather | solution.py:67
  318.3 14.5 %convolution_convert_fusion = bf16[512,2048]{1,0:T(8,128)(2,1)} fusion(bf16[512,4096]{1,0:T(8,128)(2,1)} %all-gather.3.cloned.1.call-done, bf16[4096,2048]{1,0:T(8,128)(2,1)} %all-gather.5.cloned.1.call-done), kind=kOutput, calls=%fused_computation.45 | convolution fusion | flops 8590983168 | bytes 23068672 | tf_op jit(solution)/shard_map/dot_general | solution.py:65
  332.9 3.9 copy.17
  336.8 320.4 %while.16 = (s32[]{:T(128)}, f32[32,512,64]{1,2,0:T(8,128)}, f32[32,512,64]{1,2,0:T(8,128)}, s32[32]{0:T(128)S(1)}, f32[4,32,512]{2,1,0:T(8,128)}, /*index=5*/f3...) while((s32[]{:T(128)}, f32[32,512,64]{1,2,0:T(8,128)}, ...), condition=%wide.region_3.4_spmd.clone.clone, body=%wide.region_2.3_spmd.clone.clone.sunk | while | flops 80740360 | bytes 6754623 | solution.py:103
  410.9 3.1 fusion.100
  490.9 3.1 fusion.100
  541.0 3.1 fusion.100
  561.1 3.1 fusion.100
  631.1 3.1 fusion.100
  641.1 3.1 fusion.100
  657.2 5.4 fusion.25
  662.6 11.7 %convert_bitcast_fusion = bf16[4096,2048]{0,1:T(8,128)(2,1)} fusion(bf16[512,2048]{0,1:T(8,128)(2,1)S(1)} %bitcast.146, bf16[512,4096]{1,0:T(8,128)(2,1)S(1)} %copy-done.12), kind=kOutput, calls=%fused_computation.31 | convolution fusion | flops 8598323200 | bytes 23068672 | tf_op jit(solution)/shard_map/dot_general | solution.py:163
  679.8 22.8 %collective-permute-done = bf16[32,128,64]{1,2,0:T(8,128)(2,1)S(1)} collective-permute-done((bf16[32,128,64]{1,2,0:T(8,128)(2,1)S(1)}, bf16[32,128,64]{1,2,0:T(8,128)(2,1)S(1)}, u32[]{:S(2)}, u32[]{:S(2)}) %collective-permute-start) | collective-permute-done | bytes 524320 | tf_op jit(solution)/shard_map/ppermute | solution.py:14
  703.0 40.2 %collective-permute-done.2 = bf16[32,128,64]{1,2,0:T(8,128)(2,1)S(1)} collective-permute-done((bf16[32,128,64]{1,2,0:T(8,128)(2,1)S(1)}, bf16[32,128,64]{1,2,0:T(8,128)(2,1)S(1)}, u32[]{:S(2)}, u32[]{:S(2)}) %collective-permute-start.2) | collective-permute-done | bytes 524320 | tf_op jit(solution)/shard_map/ppermute | solution.py:14
  743.9 50.4 %collective-permute-done.4 = bf16[32,128,64]{1,2,0:T(8,128)(2,1)S(1)} collective-permute-done((bf16[32,128,64]{1,2,0:T(8,128)(2,1)S(1)}, bf16[32,128,64]{1,2,0:T(8,128)(2,1)S(1)}, u32[]{:S(2)}, u32[]{:S(2)}) %collective-permute-start.4) | collective-permute-done | bytes 524320 | tf_op jit(solution)/shard_map/ppermute | solution.py:14
  794.6 7.0 fusion.26
  804.0 183.2 %reduce-scatter.2.cloned.1.call-done = bf16[512,2048]{0,1:T(8,128)(2,1)} async-done(((bf16[4096,2048]{0,1:T(8,128)(2,1)}), bf16[512,2048]{0,1:T(8,128)(2,1)}) %reduce-scatter.2.cloned.1.call-update) | async-done | bytes 2097168 | tf_op jit(solution)/shard_map/reduce_scatter | solution.py:162
  987.2 3.9 copy.26
  (297 shorter events, 270.8 us)
Async XLA Ops:
  7.2 4.5 copy-start.10
  7.2 11.1 %copy-start.5 = (bf16[512,2048]{1,0:T(8,128)(2,1)S(1)}, bf16[512,2048]{1,0:T(8,128)(2,1)}, u32[]{:S(2)}) copy-start(bf16[512,2048]{1,0:T(8,128)(2,1)} %param.19) | copy-start | bytes 6291460
  7.2 150.3 %all-gather.3.cloned.1.call-start = ((), (), s32[]{:S(2)}) async-start(), calls=%async_computation.1 | async-start | bytes 5242880 | tf_op jit(solution)/shard_map/all_gather | solution.py:54
  7.9 310.4 %all-gather.5.cloned.1.call-start = ((), (), s32[]{:S(2)}) async-start(), calls=%async_computation.2 | async-start | bytes 18874368 | tf_op jit(solution)/shard_map/all_gather | solution.py:67
  8.7 978.5 %reduce-scatter.2.cloned.1.call-start = ((), (), s32[]{:S(2)}) async-start(), calls=%async_computation.3 | async-start | bytes 18874368 | tf_op jit(solution)/shard_map/reduce_scatter | solution.py:162
  39.1 52.6 %collective-permute-start.5 = (bf16[3,32,128,64]{2,3,1,0:T(8,128)(2,1)S(1)}, bf16[3,32,128,64]{2,3,1,0:T(8,128)(2,1)S(1)}, u32[]{:S(2)}, u32[]{:S(2)}) collective-permute-start(bf16[3,32,128,64]{2,3,1,0:T(8,128)(2,1)S(1)} %get-tuple-element.191), channel_id=1, source_target_pairs={{0,4},{4,0},{8,12},{12,8},{16,20},{20,16},{24,28},{28,24},{1,5},{5... | collective-permute-start | bytes 4718600 | tf_op jit(solution)/shard_map/ppermute | solution.py:14
  41.0 50.7 %collective-permute-start.1 = (bf16[32]{0:T(256)(128)(2,1)S(1)}, bf16[32]{0:T(256)(128)(2,1)S(1)}, u32[]{:S(2)}, u32[]{:S(2)}) collective-permute-start(bf16[32]{0:T(256)(128)(2,1)S(1)} %exponential_convert_fusion), channel_id=1, source_target_pairs={{0,4},{4,0},{8,12},{12,8},{16,20},{20,16},{24,28},{28,24},{1,5},{5... | collective-permute-start | bytes 200 | tf_op jit(solution)/shard_map/ppermute | solution.py:14
  92.1 5.5 copy-start.11
  94.3 59.2 %collective-permute-start.6 = (bf16[2,32,128,64]{2,3,1,0:T(8,128)(2,1)}, bf16[2,32,128,64]{2,3,1,0:T(8,128)(2,1)}, u32[]{:S(2)}, u32[]{:S(2)}) collective-permute-start(bf16[2,32,128,64]{2,3,1,0:T(8,128)(2,1)} %get-tuple-element.189), channel_id=1, source_target_pairs={{0,8},{4,12},{8,0},{12,4},{16,24},{20,28},{24,16},{28,20},{1,9},{5... | collective-permute-start | bytes 3145736 | tf_op jit(solution)/shard_map/ppermute | solution.py:14
  105.2 48.4 %collective-permute-start.3 = (bf16[32]{0:T(256)(128)(2,1)S(1)}, bf16[32]{0:T(256)(128)(2,1)S(1)}, u32[]{:S(2)}, u32[]{:S(2)}) collective-permute-start(bf16[32]{0:T(256)(128)(2,1)S(1)} %get-tuple-element.195), channel_id=1, source_target_pairs={{0,8},{4,12},{8,0},{12,4},{16,24},{20,28},{24,16},{28,20},{1,9},{5... | collective-permute-start | bytes 200 | tf_op jit(solution)/shard_map/ppermute | solution.py:14
  105.7 50.7 %copy-start.4 = (f32[2,32,128,64]{2,3,1,0:T(8,128)S(1)}, f32[2,32,128,64]{2,3,1,0:T(8,128)}, u32[]{:S(2)}) copy-start(f32[2,32,128,64]{2,3,1,0:T(8,128)} %get-tuple-element.190) | copy-start | bytes 6291460
  157.5 499.7 %collective-permute-start.7 = (bf16[1,32,128,64]{2,3,1,0:T(8,128)(2,1)}, bf16[1,32,128,64]{2,3,1,0:T(8,128)(2,1)}, u32[]{:S(2)}, u32[]{:S(2)}) collective-permute-start(bf16[1,32,128,64]{2,3,1,0:T(8,128)(2,1)} %select_convert_fusion), channel_id=1, source_target_pairs={{0,16},{4,20},{8,24},{12,28},{16,0},{20,4},{24,8},{28,12},{1,17},{... | collective-permute-start | bytes 1572872 | tf_op jit(solution)/shard_map/ppermute | solution.py:14
  336.8 320.4 %copy-start.8 = (f32[512,128]{1,0:T(8,128)S(1)}, f32[512,128]{1,0:T(8,128)}, u32[]{:S(2)}) copy-start(f32[512,128]{1,0:T(8,128)} %convert_element_type.117) | copy-start | bytes 786436
  410.9 3.1 copy-start.7
  541.0 3.1 copy-start.7
  561.1 3.1 copy-start.7
  631.1 3.1 copy-start.7
  641.1 3.1 copy-start.7
  657.1 5.4 copy-start.12
  678.5 24.1 %collective-permute-start = (bf16[32,128,64]{1,2,0:T(8,128)(2,1)S(1)}, bf16[32,128,64]{1,2,0:T(8,128)(2,1)S(1)}, u32[]{:S(2)}, u32[]{:S(2)}) collective-permute-start(bf16[32,128,64]{1,2,0:T(8,128)(2,1)S(1)} %get-tuple-element.209), channel_id=1, source_target_pairs={{0,4},{4,0},{8,12},{12,8},{16,20},{20,16},{24,28},{28,24},{1,5},{5... | collective-permute-start | bytes 1572872 | tf_op jit(solution)/shard_map/ppermute | solution.py:14
  702.6 92.0 %copy-start.2 = (f32[32,512,64]{1,2,0:T(8,128)S(1)}, f32[32,512,64]{1,2,0:T(8,128)}, u32[]{:S(2)}) copy-start(f32[32,512,64]{1,2,0:T(8,128)} %get-tuple-element.96) | copy-start | bytes 12582916
  702.9 40.3 %collective-permute-start.2 = (bf16[32,128,64]{1,2,0:T(8,128)(2,1)S(1)}, bf16[32,128,64]{1,2,0:T(8,128)(2,1)S(1)}, u32[]{:S(2)}, u32[]{:S(2)}) collective-permute-start(bf16[32,128,64]{1,2,0:T(8,128)(2,1)S(1)} %fusion.69), channel_id=1, source_target_pairs={{0,8},{4,12},{8,0},{12,4},{16,24},{20,28},{24,16},{28,20},{1,9},{5... | collective-permute-start | bytes 1572872 | tf_op jit(solution)/shard_map/ppermute | solution.py:14
  743.9 50.5 %collective-permute-start.4 = (bf16[32,128,64]{1,2,0:T(8,128)(2,1)S(1)}, bf16[32,128,64]{1,2,0:T(8,128)(2,1)S(1)}, u32[]{:S(2)}, u32[]{:S(2)}) collective-permute-start(bf16[32,128,64]{1,2,0:T(8,128)(2,1)S(1)} %get-tuple-element.202), channel_id=1, source_target_pairs={{0,16},{4,20},{8,24},{12,28},{16,0},{20,4},{24,8},{28,12},{1,17},{... | collective-permute-start | bytes 1572872 | tf_op jit(solution)/shard_map/ppermute | solution.py:14
  801.6 189.5 %copy-start.1 = (f32[32,512]{1,0:T(8,128)S(1)}, f32[32,512]{1,0:T(8,128)}, u32[]{:S(2)}) copy-start(f32[32,512]{1,0:T(8,128)} %param.17) | copy-start | bytes 196612
  (31 other events, 88.5 us)
Sparse Core Ops, SparseCore 0:
  9.6 37.1 all-gather.2
  48.9 269.3 all-gather.4
  674.4 312.7 reduce-scatter.1
where the time goes:
time: 1010 us; the launch traced here: 998 us
  waiting for transfers between devices  557 us (55%)
  matrix products  243 us (24%)
  local copies, waits for them, and re-layouts  84.9 us (8%)
  loops' own time  62.6 us (6%)
  other arithmetic  18.5 us (2%)
  between operations  14 us (1%)
  blocking collectives  12.1 us (1%)
    ppermute x8, waiting for transfers between devices, swapped(): return lax.ppermute(value, axis, pairs)  212 us
    reduce_scatter x1, waiting for transfers between devices, per_device(): lax.psum_scatter(lax.dot_general(tok_part, values_grad, (((0,), (0,)), ((...  183 us
    all_gather x1, waiting for transfers between devices, per_device(): lax.all_gather(in_weight, 'seq', axis=0, tiled=True)  161 us
    dot_general x32, matrix products, head_terms(): lax.dot_general(weights, grad_rows, (((0,), (0,)), ((), ())), preferred_e...  97.6 us
    dot_general x32, matrix products, head_terms(): forward = jnp.dot(weights, values, preferred_element_type=jnp.float32)  93.3 us
    another operation x1, loops' own time, per_device(): local_out, local_grad = lax.map(one_head, jnp.arange(head_count))  62.6 us
    slice x32, local copies, waits for them, and re-layouts, head_terms(): gain_rows[number][:, None]  24.9 us
    dynamic_slice x32, local copies, waits for them, and re-layouts, one_head(): cum_head = cumulative[number]  23.3 us
  transfers between devices with their start and end apart: 11, of which 7 were waited for; matrix products, arithmetic and copies ran while one was open for 32% of the time, Pallas kernels for 0%

commit v1 on v0

v1 whole, which is shorter than its diff:
```python
import functools

import jax
import jax.numpy as jnp
from jax import lax
from jax.experimental import pallas as pl
from jax.experimental.pallas import tpu as pltpu
from jax.sharding import PartitionSpec as P

HEAD_DIM = 64
STATE = 128
CH = 64
TILE = 2 * CH
GROUP = 4


def swapped(value, axis, apart):
    mask = 2**apart
    pairs = [(source, source ^ mask) for source in range(lax.axis_size(axis))]
    return lax.ppermute(value, axis, pairs)


def dot32(left, right):
    return jnp.dot(left, right, preferred_element_type=jnp.float32)


def spread(cols, quantity, quantities, group, rows=slice(None)):
    parts = []
    count = rows.stop - rows.start if rows.start is not None else cols.shape[1]
    low = lax.broadcasted_iota(jnp.int32, (count, 2 * HEAD_DIM), 1) < HEAD_DIM
    for pair in range(group // 2):
        first, second = (2 * pair) * quantities + quantity, (2 * pair + 1) * quantities + quantity
        parts.append(
            jnp.where(low, cols[0, rows, first : first + 1], cols[0, rows, second : second + 1])
        )
    return jnp.concatenate(parts, axis=1)


def level_grad_kernel(names, group, read_t, grads, cols, out):
    count = len(names)
    for b in range(out.shape[0]):
        scaled = (spread(cols, names.index(("q", b)), count, group) * grads[...]).astype(jnp.bfloat16)
        out[b] = dot32(read_t[...], scaled)


def seg_state_kernel(names, group, write_t, values, cols, out):
    scaled = (spread(cols, names.index("key"), len(names), group) * values[...]).astype(jnp.bfloat16)
    out[...] = dot32(write_t[...], scaled)


def diagonal_terms(names, group, table, cols, rows, operand, rows_of, backward):
    count = len(names)
    position = slice(rows_of, rows_of + TILE)
    own = table[position, position].astype(jnp.float32)
    shape = (TILE, TILE)
    same = (lax.broadcasted_iota(jnp.int32, shape, 0) < CH) == (
        lax.broadcasted_iota(jnp.int32, shape, 1) < CH
    )
    parts = []
    for head in range(group):
        cum_col = cols[0, position, head * count : head * count + 1]
        cum_row = rows[0, 3 * head : 3 * head + 1, position]
        if backward:
            gain = jnp.where(
                same, rows[0, 3 * head + 1 : 3 * head + 2, position], rows[0, 3 * head + 2 : 3 * head + 3, position]
            )
            differ = cum_row - cum_col
        else:
            gain = jnp.where(
                same,
                cols[0, position, head * count + 1 : head * count + 2],
                cols[0, position, head * count + 2 : head * count + 3],
            )
            differ = cum_col - cum_row
        weights = (gain * jnp.exp(jnp.minimum(differ, 0.0)) * own).astype(jnp.bfloat16)
        parts.append(dot32(weights, operand[position, head * HEAD_DIM : (head + 1) * HEAD_DIM]))
    return jnp.concatenate(parts, axis=1)


def local_kernel(names, group, levels, backward, table, proj, operand, states, cols, rows, out):
    count = len(names)
    length = out.shape[0]
    tiles = length // TILE
    sums = []
    for tile in range(tiles):
        position = slice(tile * TILE, (tile + 1) * TILE)
        total = diagonal_terms(names, group, table, cols, rows, operand, tile * TILE, backward)
        if backward:
            total = total + spread(cols, names.index("key"), count, group, position) * dot32(
                proj[position, :], states[...]
            )
        else:
            for b in range(states.shape[0]):
                total = total + spread(cols, names.index(("q", b)), count, group, position) * dot32(
                    proj[position, :], states[b]
                )
        sums.append(total)
    for level in range(2, levels):
        half = CH << (level - 1)
        for start in range(0, length, 2 * half):
            lower, upper = slice(start, start + half), slice(start + half, start + 2 * half)
            source, target = (upper, lower) if backward else (lower, upper)
            inner, outer = ("r", "c") if backward else ("c", "r")
            scaled = (
                spread(cols, names.index((inner, level)), count, group, source) * operand[source, :]
            ).astype(jnp.bfloat16)
            term = spread(cols, names.index((outer, level)), count, group, target) * dot32(
                table[target, source], scaled
            )
            for step in range(half // TILE):
                at = target.start // TILE + step
                sums[at] = sums[at] + term[step * TILE : (step + 1) * TILE]
    for tile in range(tiles):
        out[tile * TILE : (tile + 1) * TILE, :] = sums[tile].astype(out.dtype)


def whole_spec(array):
    return pl.BlockSpec(array.shape, lambda i: (0,) * array.ndim)


def column_spec(array, width):
    lead = array.shape[:-1]
    return pl.BlockSpec(lead + (width,), lambda i: (0,) * len(lead) + (i,))


def group_spec(array):
    return pl.BlockSpec((1,) + array.shape[1:], lambda i: (i, 0, 0))


def call(kernel, groups, width, fixed, wide, grouped, out_shape, flops, name):
    out_lead = out_shape.shape[:-1]
    moved = sum(a.size * a.dtype.itemsize for a in (*fixed, *wide, *grouped))
    return pl.pallas_call(
        kernel,
        grid=(groups,),
        in_specs=[whole_spec(a) for a in fixed]
        + [column_spec(a, width) for a in wide]
        + [group_spec(a) for a in grouped],
        out_specs=pl.BlockSpec(out_lead + (width,), lambda i: (0,) * len(out_lead) + (i,)),
        out_shape=out_shape,
        compiler_params=pltpu.CompilerParams(vmem_limit_bytes=40 * 2**20),
        cost_estimate=pl.CostEstimate(flops=flops, bytes_accessed=moved, transcendentals=0),
        name=name,
    )(*fixed, *wide, *grouped)


def per_device(tokens, in_weight, write_proj, read_proj, log_decay, level_gain, out_grad):
    full_weight = lax.all_gather(in_weight, "seq", axis=0, tiled=True)
    both = lax.all_gather(jnp.concatenate([write_proj, read_proj], axis=1), "head", axis=0, tiled=True)
    write_rows, read_rows = both[:, :STATE], both[:, STATE:]
    full_tokens = lax.all_gather(tokens, "head", axis=0, tiled=True)
    tok_len = full_tokens.shape[0]
    head_count = log_decay.shape[0]
    columns = in_weight.shape[1]
    levels = (tok_len // CH).bit_length()
    seq_count = lax.axis_size("seq").bit_length() - 1
    me = lax.axis_index("seq")
    group = GROUP
    groups = head_count // group
    width = group * HEAD_DIM

    upper_ones = (jnp.arange(tok_len)[:, None] <= jnp.arange(tok_len)[None, :]).astype(jnp.float32)
    cumulative = jnp.dot(log_decay, upper_ones, precision=lax.Precision.HIGHEST)
    totals = cumulative[:, -1]
    all_totals = lax.all_gather(totals, "seq", axis=0, tiled=False)

    names = ["cum", "g0", "g1"]
    vectors = [cumulative, level_gain[0], level_gain[1]]
    for level in range(2, levels):
        half = CH << (level - 1)
        blocks = cumulative.reshape(head_count, tok_len // (2 * half), 2 * half)
        middle = blocks[:, :, half - 1 : half]
        after = jnp.exp(jnp.minimum(blocks - middle, 0.0)).reshape(head_count, tok_len)
        before = jnp.exp(jnp.minimum(middle - blocks, 0.0)).reshape(head_count, tok_len)
        names += [("r", level), ("c", level)]
        vectors += [level_gain[level] * after, before]
    names.append("key")
    vectors.append(jnp.exp(totals[:, None] - cumulative))
    grown = jnp.exp(cumulative)
    for b in range(seq_count):
        names.append(("q", b))
        vectors.append(level_gain[levels + b] * grown)
    names = tuple(names)
    count = len(names)
    cols = jnp.stack(vectors, axis=1).reshape(groups, group * count, tok_len).swapaxes(1, 2)
    rows = jnp.stack(vectors[:3], axis=1).reshape(groups, group * 3, tok_len)

    causal = jnp.arange(tok_len)[:, None] >= jnp.arange(tok_len)[None, :]
    scores = jnp.where(causal, dot32(read_rows, write_rows.T), 0.0).astype(jnp.bfloat16)
    scores_t = jnp.where(causal.T, dot32(write_rows, read_rows.T), 0.0).astype(jnp.bfloat16)

    work = 2 * tok_len * STATE * columns
    level_grads = call(
        functools.partial(level_grad_kernel, names, group),
        groups, width, [read_rows.T], [out_grad], [cols],
        jax.ShapeDtypeStruct((seq_count, STATE, columns), jnp.float32), seq_count * work, "level_grads",
    )

    index = jnp.arange(all_totals.shape[0])
    bit_flags = [me >> bit & 1 == 1 for bit in range(seq_count)]

    def per_column(vector):
        return jnp.repeat(vector, HEAD_DIM)[None, :]

    own_decays, partner_decays = [], []
    for bit in range(seq_count):
        for found, block in ((own_decays, me >> bit), (partner_decays, (me >> bit) ^ 1)):
            inside = (index >> bit == block)[:, None]
            found.append(per_column(jnp.exp(jnp.sum(jnp.where(inside, all_totals, 0.0), axis=0))))

    pending = [jnp.where(bit_flags[bit], level_grads[bit], 0.0) for bit in range(seq_count)]
    suffix = jnp.ones((1, columns), jnp.float32)
    state_grad = jnp.zeros((STATE, columns), jnp.float32)
    for bit in range(seq_count):
        partner = swapped(jnp.stack(pending[bit:]).astype(jnp.bfloat16), "seq", bit).astype(jnp.float32)
        is_upper = bit_flags[bit]
        state_grad = state_grad + jnp.where(is_upper, 0.0, suffix * partner[0])
        for later in range(bit + 1, seq_count):
            rest, other = pending[later], partner[later - bit]
            pending[later] = jnp.where(
                is_upper, other + partner_decays[bit] * rest, rest + own_decays[bit] * other
            )
        suffix = jnp.where(is_upper, suffix, suffix * partner_decays[bit])

    local_work = work + 2 * tok_len * tok_len * columns
    values_grad = call(
        functools.partial(local_kernel, names, group, levels, True),
        groups, width, [scores_t, write_rows], [out_grad, state_grad.astype(jnp.bfloat16)], [cols, rows],
        jax.ShapeDtypeStruct((tok_len, columns), jnp.bfloat16), local_work, "backward",
    )
    weight_grad = lax.psum_scatter(
        lax.dot_general(
            full_tokens, values_grad, (((0,), (0,)), ((), ())), preferred_element_type=jnp.float32
        ).astype(jnp.bfloat16),
        "seq", scatter_dimension=0, tiled=True,
    )

    values = dot32(full_tokens, full_weight).astype(jnp.bfloat16)
    block_state = call(
        functools.partial(seg_state_kernel, names, group),
        groups, width, [write_rows.T], [values], [cols],
        jax.ShapeDtypeStruct((STATE, columns), jnp.float32), work, "seg_state",
    )
    prefix = jnp.ones((1, columns), jnp.float32)
    buckets = []
    for bit in range(seq_count):
        partner = swapped(block_state.astype(jnp.bfloat16), "seq", bit).astype(jnp.float32)
        is_upper = bit_flags[bit]
        buckets.append(jnp.where(is_upper, prefix * partner, 0.0).astype(jnp.bfloat16))
        block_state = jnp.where(
            is_upper,
            own_decays[bit] * partner + block_state,
            partner_decays[bit] * block_state + partner,
        )
        prefix = jnp.where(is_upper, partner_decays[bit] * prefix, prefix)
    layer_out = call(
        functools.partial(local_kernel, names, group, levels, False),
        groups, width, [scores, read_rows], [values, jnp.stack(buckets)], [cols, rows],
        jax.ShapeDtypeStruct((tok_len, columns), jnp.bfloat16), local_work, "forward",
    )
    return (layer_out, weight_grad)


def solution(mesh):
    in_specs = (
        P(("seq", "head"), None),
        P("seq", "head"),
        P(("seq", "head"), None),
        P(("seq", "head"), None),
        P("head", "seq"),
        P(None, "head", "seq"),
        P("seq", "head"),
    )
    out_specs = (P("seq", "head"), P("seq", "head"))
    return jax.shard_map(
        per_device, mesh=mesh, in_specs=in_specs, out_specs=out_specs, check_vma=False
    )
```

time: 1010 us -> 644 us (0.64); the launches traced: 998 us -> 644 us
  matrix products: 243 us -> 29.4 us
  waiting for transfers between devices: 557 us -> 433 us
  local copies, waits for them, and re-layouts: 84.9 us -> 15.3 us
  Pallas kernels: 0 us -> 64.9 us
  loops' own time: 62.6 us -> 0 us
  blocking collectives: 12.1 us -> 66.4 us
    dot_general x71 -> x5, matrix products: 243 us -> 29.4 us  [the longest x1 14.9 us: per_device(): lax.dot_general(full_tokens, values_grad, (((0,), (0,)), ((), ())), prefe...]
    all_gather x2, waiting for transfers between devices: 161 us -> 64.1 us  [the longest x1 64 us: per_device(): full_weight = lax.all_gather(in_weight, 'seq', axis=0, tiled=True)]
    pallas_call x0 -> x4, Pallas kernels: none -> 64.9 us  [call(): pl.pallas_call(kernel, grid=(groups,), in_specs=[whole_spec(a) for a in f...]
    another operation x1 -> x0, loops' own time: 62.6 us -> none  [per_device(): local_out, local_grad = lax.map(one_head, jnp.arange(head_count))]
    unnamed x0 -> x1, blocking collectives: none -> 59.2 us
    dynamic_slice x64 -> x0, local copies, waits for them, and re-layouts: 41.9 us -> none  [the longest x32 23.3 us: one_head(): cum_head = cumulative[number]]
    reduce_scatter x1, waiting for transfers between devices: 183 us -> 149 us  [per_device(): lax.psum_scatter(lax.dot_general(full_tokens, values_grad, (((0,), (0,)),...]
    slice x33 -> x2, local copies, waits for them, and re-layouts: 26.5 us -> 0.27 us  [per_device(): middle = blocks[:, :, half - 1:half]]
  transfers between devices with their start and end apart: 11 -> 9, of which waited for: 7 -> 7; matrix products, arithmetic and copies ran while one was open for 32% -> 7% of each run, Pallas kernels for 0% -> 10%
where the time goes in v1:
time: 644 us
  waiting for transfers between devices  433 us (67%)
  blocking collectives  66.4 us (10%)
  Pallas kernels  64.9 us (10%)
  matrix products  29.4 us (5%)
  local copies, waits for them, and re-layouts  15.3 us (2%)
  between operations  14.9 us (2%)
  other arithmetic  12.9 us (2%)
  starting transfers between devices  6.94 us (1%)
    ppermute x6, waiting for transfers between devices, swapped(): return lax.ppermute(value, axis, pairs)  219 us
    reduce_scatter x1, waiting for transfers between devices, per_device(): lax.psum_scatter(lax.dot_general(full_tokens, values_grad, (((0,), (0,)),...  149 us
    pallas_call x4, Pallas kernels, call(): pl.pallas_call(kernel, grid=(groups,), in_specs=[whole_spec(a) for a in f...  64.9 us
    all_gather x1, waiting for transfers between devices, per_device(): full_weight = lax.all_gather(in_weight, 'seq', axis=0, tiled=True)  64 us
    unnamed x1, blocking collectives  59.2 us
    dot_general x1, matrix products, per_device(): lax.dot_general(full_tokens, values_grad, (((0,), (0,)), ((), ())), prefe...  14.9 us
    dot_general x3, matrix products, dot32(): return jnp.dot(left, right, preferred_element_type=jnp.float32)  14.2 us
  transfers between devices with their start and end apart: 9, of which 7 were waited for; matrix products, arithmetic and copies ran while one was open for 7% of the time, Pallas kernels for 10%

profile of v1, /device:TPU:0, one launch (start us, length us, event | category | flops | bytes accessed | tf_op | source)
XLA Modules:
  0.0 643.5 jit_solution(3236066067557510546)
XLA Ops:
  8.8 7.2 %all_gather.12 = bf16[512,256]{1,0:T(8,128)(2,1)S(1)} all-gather(bf16[128,256]{1,0:T(8,128)(2,1)S(1)} %pad_maximum_fusion.4), channel_id=1, replica_groups=mesh['seq'=8,'head'=4] {'head'}, dimensions={0}, use_global_device_ids=true | all-gather | bytes 327680 | tf_op jit(solution)/shard_map/all_gather | solution.py:149
  19.7 1.7 copy-done.4
  21.5 9.4 %level_grads.1 = f32[3,128,2048]{2,1,0:T(8,128)S(1)} custom-call(bf16[128,512]{1,0:T(8,128)(2,1)S(1)} %copy.29.read_t, bf16[512,2048]{1,0:T(8,128)(2,1)S(1)} %copy-done.4, f32[8,512,44]{2,1,0:T(8,128)S(1)} %bitcast.97), custom_call_target="tpu_custom_call" | custom-call | flops 805306368 | bytes 2949120 | tf_op jit(solution)/shard_map/level_grads/pallas_call | solution.py:133
  31.2 1.7 pad_maximum_fusion.1
  33.1 1.6 collective-permute-start.3
  36.1 59.2 %all-reduce = f32[256]{0:T(256)S(1)} all-reduce(f32[256]{0:T(256)S(1)} %dynamic-update-slice), channel_id=2, replica_groups=mesh['seq'=8,'head'=4] {'seq'}, use_global_device_ids=true, to_apply=%add | all-reduce | flops 256 | bytes 2048
  95.8 1.9 convert_element_type.72
  102.2 49.7 %collective-permute-done.4 = bf16[2,128,2048]{2,1,0:T(8,128)(2,1)S(1)} collective-permute-done((bf16[2,128,2048]{2,1,0:T(8,128)(2,1)}, bf16[2,128,2048]{2,1,0:T(8,128)(2,1)S(1)}, u32[]{:S(2)}, u32[]{:S(2)}) %collective-permute-start.4) | collective-permute-done | bytes 1048608 | tf_op jit(solution)/shard_map/ppermute | solution.py:20
  152.2 3.5 select_convert_fusion
  156.9 58.3 %collective-permute-done.5 = bf16[1,128,2048]{2,1,0:T(8,128)(2,1)} collective-permute-done((bf16[1,128,2048]{2,1,0:T(8,128)(2,1)}, bf16[1,128,2048]{2,1,0:T(8,128)(2,1)}, u32[]{:S(2)}, u32[]{:S(2)}) %collective-permute-start.5) | collective-permute-done | bytes 524320 | tf_op jit(solution)/shard_map/ppermute | solution.py:20
  215.2 2.0 fusion.14.states
  217.2 18.4 %backward.1 = bf16[512,2048]{1,0:T(8,128)(2,1)S(1)} custom-call(bf16[512,512]{1,0:T(8,128)(2,1)S(1)} %fusion.1.table, bf16[512,128]{1,0:T(8,128)(2,1)S(1)} %get-tuple-element.28.proj, bf16[512,2048]{1,0:T(8,128)(2,1)S(1)} %copy-done.5, bf16[128,2048]{1,0:T(8,128)(2,1)S(1)} %fusion.14.states, f32[8,512,44]{2,1,0:T(8,128)S(1)} %bitcast.98, ...), custom_call_target="tpu_custom_call" | custom-call | flops 1342177280 | bytes 4194304 | tf_op jit(solution)/shard_map/backward/pallas_call | solution.py:133
  236.9 14.9 %convert_bitcast_fusion = bf16[4096,2048]{0,1:T(8,128)(2,1)} fusion(bf16[512,2048]{1,0:T(8,128)(2,1)} %copy-done.6, bf16[512,4096]{1,0:T(8,128)(2,1)} %all-gather.4.cloned.1.call-done), kind=kOutput, calls=%fused_computation | convolution fusion | flops 8598323200 | bytes 23068672 | tf_op jit(solution)/shard_map/dot_general | solution.py:232
  252.9 64.0 %all-gather.6.cloned.1.call-done = bf16[4096,2048]{1,0:T(8,128)(2,1)} async-done(((bf16[512,2048]{1,0:T(8,128)(2,1)}), bf16[4096,2048]{1,0:T(8,128)(2,1)}) %all-gather.6.cloned.1.call-update) | async-done | bytes 16777232 | tf_op jit(solution)/shard_map/all_gather | solution.py:148
  316.9 13.6 %convolution_convert_fusion.values.operand = bf16[512,2048]{1,0:T(8,128)(2,1)S(1)} fusion(bf16[512,4096]{1,0:T(8,128)(2,1)} %all-gather.4.cloned.1.call-done, bf16[4096,2048]{1,0:T(8,128)(2,1)} %all-gather.6.cloned.1.call-done), kind=kOutput, calls=%fused_computation.1 | convolution fusion | flops 8590983168 | bytes 23068672 | tf_op jit(solution)/shard_map/dot_general | solution.py:24
  330.5 4.9 seg_state.1
  335.4 1.6 collective-permute-start
  337.0 14.7 %collective-permute-done = bf16[128,2048]{1,0:T(8,128)(2,1)S(1)} collective-permute-done((bf16[128,2048]{1,0:T(8,128)(2,1)S(1)}, bf16[128,2048]{1,0:T(8,128)(2,1)S(1)}, u32[]{:S(2)}, u32[]{:S(2)}) %collective-permute-start) | collective-permute-done | bytes 524320 | tf_op jit(solution)/shard_map/ppermute | solution.py:20
  353.5 40.7 %collective-permute-done.1 = bf16[128,2048]{1,0:T(8,128)(2,1)S(1)} collective-permute-done((bf16[128,2048]{1,0:T(8,128)(2,1)S(1)}, bf16[128,2048]{1,0:T(8,128)(2,1)S(1)}, u32[]{:S(2)}, u32[]{:S(2)}) %collective-permute-start.1) | collective-permute-done | bytes 524320 | tf_op jit(solution)/shard_map/ppermute | solution.py:20
  394.8 1.6 collective-permute-start.2
  396.6 55.2 %collective-permute-done.2 = bf16[128,2048]{1,0:T(8,128)(2,1)S(1)} collective-permute-done((bf16[128,2048]{1,0:T(8,128)(2,1)S(1)}, bf16[128,2048]{1,0:T(8,128)(2,1)S(1)}, u32[]{:S(2)}, u32[]{:S(2)}) %collective-permute-start.2) | collective-permute-done | bytes 524320 | tf_op jit(solution)/shard_map/ppermute | solution.py:20
  452.2 32.3 %forward.1 = bf16[512,2048]{1,0:T(8,128)(2,1)} custom-call(bf16[512,512]{1,0:T(8,128)(2,1)S(1)} %fusion.table, bf16[512,128]{1,0:T(8,128)(2,1)S(1)} %get-tuple-element.29.proj, bf16[512,2048]{1,0:T(8,128)(2,1)S(1)} %convolution_convert_fusion.values.operand, bf16[3,128,2048]{2,1,0:T(8,128)(2,1)S(1)} %pad_maximum_fusion.states, f32[8,512,44]{2,1,0:T(8,128)S(1)} %bitcast.100, ...), custom_call_target="tpu_custom_call" | custom-call | flops 1342177280 | bytes 5242880 | tf_op jit(solution)/shard_map/forward/pallas_call | solution.py:133
  484.5 148.6 %reduce-scatter.2.cloned.1.call-done = bf16[512,2048]{0,1:T(8,128)(2,1)} async-done(((bf16[4096,2048]{0,1:T(8,128)(2,1)}), bf16[512,2048]{0,1:T(8,128)(2,1)}) %reduce-scatter.2.cloned.1.call-update) | async-done | bytes 2097168 | tf_op jit(solution)/shard_map/reduce_scatter | solution.py:231
  633.1 3.9 copy.30
  (103 shorter events, 18.0 us)
Async XLA Ops:
  7.2 9.7 %copy-start = (f32[32,512]{1,0:T(8,128)S(1)}, f32[32,512]{1,0:T(8,128)}, u32[]{:S(2)}) copy-start(f32[32,512]{1,0:T(8,128)} %param.11) | copy-start | bytes 196612
  7.2 1.6 copy-start.13
  7.2 1.6 copy-start.14
  7.2 229.7 %all-gather.4.cloned.1.call-start = ((), (), s32[]{:S(2)}) async-start(), calls=%async_computation.1 | async-start | bytes 5242880 | tf_op jit(solution)/shard_map/all_gather | solution.py:151
  7.9 10.1 %copy-start.11 = (f32[7,32,512]{2,1,0:T(8,128)S(1)}, f32[7,32,512]{2,1,0:T(8,128)}, u32[]{:S(2)}) copy-start(f32[7,32,512]{2,1,0:T(8,128)} %param.12) | copy-start | bytes 1376260
  7.9 309.0 %all-gather.6.cloned.1.call-start = ((), (), s32[]{:S(2)}) async-start(), calls=%async_computation.2 | async-start | bytes 18874368 | tf_op jit(solution)/shard_map/all_gather | solution.py:148
  8.7 624.4 %reduce-scatter.2.cloned.1.call-start = ((), (), s32[]{:S(2)}) async-start(), calls=%async_computation.3 | async-start | bytes 18874368 | tf_op jit(solution)/shard_map/reduce_scatter | solution.py:231
  16.0 2.4 copy-start.9
  19.7 1.7 copy-start.4
  30.9 2.2 copy-start.2
  31.2 3.4 copy-start.15
  33.1 62.8 %collective-permute-start.3 = (bf16[3,128,2048]{2,1,0:T(8,128)(2,1)}, bf16[3,128,2048]{2,1,0:T(8,128)(2,1)}, u32[]{:S(2)}, u32[]{:S(2)}) collective-permute-start(bf16[3,128,2048]{2,1,0:T(8,128)(2,1)} %pad_maximum_fusion.1), channel_id=1, source_target_pairs={{0,4},{4,0},{8,12},{12,8},{16,20},{20,16},{24,28},{28,24},{1,5},{5... | collective-permute-start | bytes 4718600 | tf_op jit(solution)/shard_map/ppermute | solution.py:20
  95.8 2.4 copy-start.3
  98.2 1.7 copy-start.7
  101.0 50.9 %collective-permute-start.4 = (bf16[2,128,2048]{2,1,0:T(8,128)(2,1)}, bf16[2,128,2048]{2,1,0:T(8,128)(2,1)S(1)}, u32[]{:S(2)}, u32[]{:S(2)}) collective-permute-start(bf16[2,128,2048]{2,1,0:T(8,128)(2,1)} %pad_maximum_fusion.2), channel_id=1, source_target_pairs={{0,8},{4,12},{8,0},{12,4},{16,24},{20,28},{24,16},{28,20},{1,9},{5... | collective-permute-start | bytes 3145736 | tf_op jit(solution)/shard_map/ppermute | solution.py:20
  152.1 4.1 copy-start.8
  152.2 4.4 copy-start.10
  155.7 59.5 %collective-permute-start.5 = (bf16[1,128,2048]{2,1,0:T(8,128)(2,1)}, bf16[1,128,2048]{2,1,0:T(8,128)(2,1)}, u32[]{:S(2)}, u32[]{:S(2)}) collective-permute-start(bf16[1,128,2048]{2,1,0:T(8,128)(2,1)} %select_convert_fusion), channel_id=1, source_target_pairs={{0,16},{4,20},{8,24},{12,28},{16,0},{20,4},{24,8},{28,12},{1,17},{... | collective-permute-start | bytes 1572872 | tf_op jit(solution)/shard_map/ppermute | solution.py:20
  156.6 60.7 %copy-start.5 = (bf16[512,2048]{1,0:T(8,128)(2,1)S(1)}, bf16[512,2048]{1,0:T(8,128)(2,1)}, u32[]{:S(2)}) copy-start(bf16[512,2048]{1,0:T(8,128)(2,1)} %operand.1) | copy-start | bytes 6291460
  235.6 1.3 copy-start.6
  335.4 16.3 %collective-permute-start = (bf16[128,2048]{1,0:T(8,128)(2,1)S(1)}, bf16[128,2048]{1,0:T(8,128)(2,1)S(1)}, u32[]{:S(2)}, u32[]{:S(2)}) collective-permute-start(bf16[128,2048]{1,0:T(8,128)(2,1)S(1)} %convert_element_type.62), channel_id=1, source_target_pairs={{0,4},{4,0},{8,12},{12,8},{16,20},{20,16},{24,28},{28,24},{1,5},{5... | collective-permute-start | bytes 1572872 | tf_op jit(solution)/shard_map/ppermute | solution.py:20
  352.0 42.2 %collective-permute-start.1 = (bf16[128,2048]{1,0:T(8,128)(2,1)S(1)}, bf16[128,2048]{1,0:T(8,128)(2,1)S(1)}, u32[]{:S(2)}, u32[]{:S(2)}) collective-permute-start(bf16[128,2048]{1,0:T(8,128)(2,1)S(1)} %fusion.24), channel_id=1, source_target_pairs={{0,8},{4,12},{8,0},{12,4},{16,24},{20,28},{24,16},{28,20},{1,9},{5... | collective-permute-start | bytes 1572872 | tf_op jit(solution)/shard_map/ppermute | solution.py:20
  394.8 57.1 %collective-permute-start.2 = (bf16[128,2048]{1,0:T(8,128)(2,1)S(1)}, bf16[128,2048]{1,0:T(8,128)(2,1)S(1)}, u32[]{:S(2)}, u32[]{:S(2)}) collective-permute-start(bf16[128,2048]{1,0:T(8,128)(2,1)S(1)} %get-tuple-element.22), channel_id=1, source_target_pairs={{0,16},{4,20},{8,24},{12,28},{16,0},{20,4},{24,8},{28,12},{1,17},{... | collective-permute-start | bytes 1572872 | tf_op jit(solution)/shard_map/ppermute | solution.py:20
  452.2 184.8 %copy-start.1 = (f32[32,512]{1,0:T(8,128)S(1)}, f32[32,512]{1,0:T(8,128)}, u32[]{:S(2)}) copy-start(f32[32,512]{1,0:T(8,128)} %param.11) | copy-start | bytes 196612
  (1 other events, 0.9 us)
Sparse Core Ops, SparseCore 0:
  9.6 37.1 all-gather.3
  48.9 267.9 all-gather.5
  320.7 312.3 reduce-scatter.1

commit v2 on v1

--- a/solution.py
+++ b/solution.py
@@ -114,6 +114,44 @@
         out[tile * TILE : (tile + 1) * TILE, :] = sums[tile].astype(out.dtype)
 
 
+def bit_orders(bits):
+    straight = list(range(bits))
+    turned = straight[1:2] + straight[:1] + straight[2:]
+    return [turned, straight, straight, straight]
+
+
+def gathered(block, order):
+    have = [([0], block)]
+    for bit in reversed(order):
+        have += [([r ^ 1 << bit for r in marks], swapped(part, "seq", bit)) for marks, part in have]
+    return have
+
+
+def scattered(blocks_t, grads, order):
+    half = blocks_t.shape[1] // 2
+
+    def product(part):
+        return lax.dot_general(
+            part, grads, (((0,), (0,)), ((), ())), preferred_element_type=jnp.float32
+        ).astype(jnp.bfloat16)
+
+    send, keep = product(blocks_t[:, half:]), product(blocks_t[:, :half])
+    for step, bit in enumerate(order):
+        arrived = swapped(send, "seq", bit)
+        total = keep.astype(jnp.float32) + arrived.astype(jnp.float32)
+        half = total.shape[0] // 2
+        if step + 1 == len(order):
+            return total.astype(jnp.bfloat16)
+        keep, send = total[:half], total[half:].astype(jnp.bfloat16)
+
+
+def marks_of(order):
+    marks = [0]
+    for bit in reversed(order):
+        marks = marks + [r | 1 << bit for r in marks]
+    return marks
+
+
 def whole_spec(array):
     return pl.BlockSpec(array.shape, lambda i: (0,) * array.ndim)
 
@@ -145,7 +183,9 @@
 
 
 def per_device(tokens, in_weight, write_proj, read_proj, log_decay, level_gain, out_grad):
-    full_weight = lax.all_gather(in_weight, "seq", axis=0, tiled=True)
+    orders = bit_orders(lax.axis_size("seq").bit_length() - 1)
+    chunk = in_weight.shape[1] // len(orders)
+    pieces = [gathered(in_weight[:, i * chunk : (i + 1) * chunk], order) for i, order in enumerate(orders)]
     both = lax.all_gather(jnp.concatenate([write_proj, read_proj], axis=1), "head", axis=0, tiled=True)
     write_rows, read_rows = both[:, :STATE], both[:, STATE:]
     full_tokens = lax.all_gather(tokens, "head", axis=0, tiled=True)
@@ -228,14 +268,26 @@
         groups, width, [scores_t, write_rows], [out_grad, state_grad.astype(jnp.bfloat16)], [cols, rows],
         jax.ShapeDtypeStruct((tok_len, columns), jnp.bfloat16), local_work, "backward",
     )
-    weight_grad = lax.psum_scatter(
-        lax.dot_general(
-            full_tokens, values_grad, (((0,), (0,)), ((), ())), preferred_element_type=jnp.float32
-        ).astype(jnp.bfloat16),
-        "seq", scatter_dimension=0, tiled=True,
-    )
-
-    values = dot32(full_tokens, full_weight).astype(jnp.bfloat16)
+    depth = in_weight.shape[0]
+    blocks = [
+        lax.dynamic_slice_in_dim(full_tokens, (me ^ r) * depth, depth, axis=1)
+        for r in range(lax.axis_size("seq"))
+    ]
+    parts = []
+    for i, order in enumerate(orders):
+        marks = marks_of(order)
+        ordered = jnp.concatenate([blocks[r] for r in marks], axis=1)
+        parts.append(scattered(ordered, values_grad[:, i * chunk : (i + 1) * chunk], order))
+    weight_grad = jnp.concatenate(parts, axis=1)
+
+    chunks = []
+    for have in pieces:
+        total = 0.0
+        for marks, part in have:
+            for k, r in enumerate(marks):
+                total = total + dot32(blocks[r], part[k * depth : (k + 1) * depth])
+        chunks.append(total.astype(jnp.bfloat16))
+    values = jnp.concatenate(chunks, axis=1)
     block_state = call(
         functools.partial(seg_state_kernel, names, group),
         groups, width, [write_rows.T], [values], [cols],

time: 644 us -> 607 us (0.943)
  waiting for transfers between devices: 433 us -> 346 us
  starting transfers between devices: 6.94 us -> 42.8 us
    reduce_scatter x1 -> x0, waiting for transfers between devices: 149 us -> none  [per_device(): lax.psum_scatter(lax.dot_general(full_tokens, values_grad, (((0,), (0,)),...]
    ppermute x6 -> x46, waiting for transfers between devices: 219 us -> 345 us  [swapped(): return lax.ppermute(value, axis, pairs)]
    all_gather x1 -> x0, waiting for transfers between devices: 64 us -> none  [per_device(): full_weight = lax.all_gather(in_weight, 'seq', axis=0, tiled=True)]
    ppermute x6 -> x46, starting transfers between devices: 6.83 us -> 42.8 us  [swapped(): return lax.ppermute(value, axis, pairs)]
    dot_general x3 -> x34, matrix products: 14.2 us -> 20.8 us  [dot32(): return jnp.dot(left, right, preferred_element_type=jnp.float32)]
    dot_general x1 -> x8, matrix products: 14.9 us -> 14.7 us  [product(): lax.dot_general(part, grads, (((0,), (0,)), ((), ())), preferred_element_...]
  transfers between devices with their start and end apart: 9 -> 47, of which waited for: 7 -> 22; matrix products, arithmetic and copies ran while one was open for 7% -> 10% of each run, Pallas kernels for 10% -> 11%
where the time goes in v2:
time: 607 us; the launch traced here: 602 us
  waiting for transfers between devices  346 us (57%)
  Pallas kernels  65.1 us (11%)
  blocking collectives  60.1 us (10%)
  starting transfers between devices  42.8 us (7%)
  matrix products  35.8 us (6%)
  local copies, waits for them, and re-layouts  21 us (3%)
  between operations  16.2 us (3%)
  other arithmetic  15.7 us (3%)
    ppermute x46, waiting for transfers between devices, swapped(): return lax.ppermute(value, axis, pairs)  345 us
    pallas_call x4, Pallas kernels, call(): pl.pallas_call(kernel, grid=(groups,), in_specs=[whole_spec(a) for a in f...  65.1 us
    unnamed x1, blocking collectives  52.8 us
    ppermute x46, starting transfers between devices, swapped(): return lax.ppermute(value, axis, pairs)  42.8 us
    dot_general x34, matrix products, dot32(): return jnp.dot(left, right, preferred_element_type=jnp.float32)  20.8 us
    dot_general x8, matrix products, product(): lax.dot_general(part, grads, (((0,), (0,)), ((), ())), preferred_element_...  14.7 us
  transfers between devices with their start and end apart: 47, of which 22 were waited for; matrix products, arithmetic and copies ran while one was open for 10% of the time, Pallas kernels for 11%

profile of v2, /device:TPU:0, one launch (start us, length us, event | category | flops | bytes accessed | tf_op | source)
XLA Modules:
  0.0 602.3 jit_solution(1536495684849563199)
XLA Ops:
  12.5 7.2 %all_gather.9 = bf16[512,256]{1,0:T(8,128)(2,1)S(1)} all-gather(bf16[128,256]{1,0:T(8,128)(2,1)S(1)} %pad_maximum_fusion.14), channel_id=1, replica_groups=mesh['seq'=8,'head'=4] {'head'}, dimensions={0}, use_global_device_ids=true | all-gather | bytes 327680 | tf_op jit(solution)/shard_map/all_gather | solution.py:189
  21.9 9.4 %level_grads.1 = f32[3,128,2048]{2,1,0:T(8,128)S(1)} custom-call(bf16[128,512]{1,0:T(8,128)(2,1)S(1)} %copy.133.read_t, bf16[512,2048]{1,0:T(8,128)(2,1)S(1)} %copy-done.4, f32[8,512,44]{2,1,0:T(8,128)S(1)} %bitcast.151), custom_call_target="tpu_custom_call" | custom-call | flops 805306368 | bytes 2949120 | tf_op jit(solution)/shard_map/level_grads/pallas_call | solution.py:171
  43.3 52.8 %all-reduce = f32[256]{0:T(256)S(1)} all-reduce(f32[256]{0:T(256)S(1)} %dynamic-update-slice), channel_id=2, replica_groups=mesh['seq'=8,'head'=4] {'seq'}, use_global_device_ids=true, to_apply=%add | all-reduce | flops 256 | bytes 2048
  106.1 20.0 %collective-permute-done.32 = bf16[2,128,2048]{2,1,0:T(8,128)(2,1)} collective-permute-done((bf16[2,128,2048]{2,1,0:T(8,128)(2,1)}, bf16[2,128,2048]{2,1,0:T(8,128)(2,1)}, u32[]{:S(2)}, u32[]{:S(2)}) %collective-permute-start.32) | collective-permute-done | bytes 1048608 | tf_op jit(solution)/shard_map/ppermute | solution.py:20
  142.5 13.3 %collective-permute-done.2 = bf16[512,512]{1,0:T(8,128)(2,1)S(1)} collective-permute-done((bf16[512,512]{1,0:T(8,128)(2,1)}, bf16[512,512]{1,0:T(8,128)(2,1)S(1)}, u32[]{:S(2)}, u32[]{:S(2)}) %collective-permute-start.2) | collective-permute-done | bytes 524320 | tf_op jit(solution)/shard_map/ppermute | solution.py:20
  160.3 12.2 %collective-permute-done.5 = bf16[512,512]{1,0:T(8,128)(2,1)S(1)} collective-permute-done((bf16[512,512]{1,0:T(8,128)(2,1)}, bf16[512,512]{1,0:T(8,128)(2,1)S(1)}, u32[]{:S(2)}, u32[]{:S(2)}) %collective-permute-start.5) | collective-permute-done | bytes 524320 | tf_op jit(solution)/shard_map/ppermute | solution.py:20
  172.9 10.8 %collective-permute-done.4 = bf16[512,512]{1,0:T(8,128)(2,1)S(1)} collective-permute-done((bf16[512,512]{1,0:T(8,128)(2,1)}, bf16[512,512]{1,0:T(8,128)(2,1)S(1)}, u32[]{:S(2)}, u32[]{:S(2)}) %collective-permute-start.4) | collective-permute-done | bytes 524320 | tf_op jit(solution)/shard_map/ppermute | solution.py:20
  191.9 16.8 %collective-permute-done.12 = bf16[512,512]{1,0:T(8,128)(2,1)S(1)} collective-permute-done((bf16[512,512]{1,0:T(8,128)(2,1)}, bf16[512,512]{1,0:T(8,128)(2,1)S(1)}, u32[]{:S(2)}, u32[]{:S(2)}) %collective-permute-start.12) | collective-permute-done | bytes 524320 | tf_op jit(solution)/shard_map/ppermute | solution.py:20
  210.1 7.3 %collective-permute-done.9 = bf16[512,512]{1,0:T(8,128)(2,1)S(1)} collective-permute-done((bf16[512,512]{1,0:T(8,128)(2,1)}, bf16[512,512]{1,0:T(8,128)(2,1)S(1)}, u32[]{:S(2)}, u32[]{:S(2)}) %collective-permute-start.9) | collective-permute-done | bytes 524320 | tf_op jit(solution)/shard_map/ppermute | solution.py:20
  227.0 18.5 %collective-permute-done.19 = bf16[512,512]{1,0:T(8,128)(2,1)S(1)} collective-permute-done((bf16[512,512]{1,0:T(8,128)(2,1)S(1)}, bf16[512,512]{1,0:T(8,128)(2,1)S(1)}, u32[]{:S(2)}, u32[]{:S(2)}) %collective-permute-start.19) | collective-permute-done | bytes 524320 | tf_op jit(solution)/shard_map/ppermute | solution.py:20
  248.9 7.9 %collective-permute-done.18 = bf16[512,512]{1,0:T(8,128)(2,1)S(1)} collective-permute-done((bf16[512,512]{1,0:T(8,128)(2,1)S(1)}, bf16[512,512]{1,0:T(8,128)(2,1)S(1)}, u32[]{:S(2)}, u32[]{:S(2)}) %collective-permute-start.18) | collective-permute-done | bytes 524320 | tf_op jit(solution)/shard_map/ppermute | solution.py:20
  269.6 20.9 %collective-permute-done.13 = bf16[512,512]{1,0:T(8,128)(2,1)S(1)} collective-permute-done((bf16[512,512]{1,0:T(8,128)(2,1)S(1)}, bf16[512,512]{1,0:T(8,128)(2,1)S(1)}, u32[]{:S(2)}, u32[]{:S(2)}) %collective-permute-start.13) | collective-permute-done | bytes 524320 | tf_op jit(solution)/shard_map/ppermute | solution.py:20
  291.5 10.3 %collective-permute-done.20 = bf16[512,512]{1,0:T(8,128)(2,1)S(1)} collective-permute-done((bf16[512,512]{1,0:T(8,128)(2,1)S(1)}, bf16[512,512]{1,0:T(8,128)(2,1)S(1)}, u32[]{:S(2)}, u32[]{:S(2)}) %collective-permute-start.20) | collective-permute-done | bytes 524320 | tf_op jit(solution)/shard_map/ppermute | solution.py:20
  303.3 8.4 %collective-permute-done.27 = bf16[512,512]{1,0:T(8,128)(2,1)S(1)} collective-permute-done((bf16[512,512]{1,0:T(8,128)(2,1)S(1)}, bf16[512,512]{1,0:T(8,128)(2,1)S(1)}, u32[]{:S(2)}, u32[]{:S(2)}) %collective-permute-start.27) | collective-permute-done | bytes 524320 | tf_op jit(solution)/shard_map/ppermute | solution.py:20
  320.0 18.4 %backward.1 = bf16[512,2048]{1,0:T(8,128)(2,1)S(1)} custom-call(bf16[512,512]{1,0:T(8,128)(2,1)S(1)} %copy-done.6, bf16[512,128]{1,0:T(8,128)(2,1)S(1)} %get-tuple-element.40.proj, bf16[512,2048]{1,0:T(8,128)(2,1)S(1)} %copy-done.5, bf16[128,2048]{1,0:T(8,128)(2,1)S(1)} %fusion.37.states, f32[8,512,44]{2,1,0:T(8,128)S(1)} %bitcast.153, ...), custom_call_target="tpu_custom_call" | custom-call | flops 1342177280 | bytes 4194304 | tf_op jit(solution)/shard_map/backward/pallas_call | solution.py:171
  344.5 14.6 %collective-permute-done.29 = bf16[128,2048]{1,0:T(8,128)(2,1)S(1)} collective-permute-done((bf16[128,2048]{1,0:T(8,128)(2,1)S(1)}, bf16[128,2048]{1,0:T(8,128)(2,1)S(1)}, u32[]{:S(2)}, u32[]{:S(2)}) %collective-permute-start.29) | collective-permute-done | bytes 524320 | tf_op jit(solution)/shard_map/ppermute | solution.py:20
  367.4 37.8 %collective-permute-done.30 = bf16[128,2048]{1,0:T(8,128)(2,1)S(1)} collective-permute-done((bf16[128,2048]{1,0:T(8,128)(2,1)S(1)}, bf16[128,2048]{1,0:T(8,128)(2,1)S(1)}, u32[]{:S(2)}, u32[]{:S(2)}) %collective-permute-start.30) | collective-permute-done | bytes 524320 | tf_op jit(solution)/shard_map/ppermute | solution.py:20
  405.5 32.5 %forward.1 = bf16[512,2048]{1,0:T(8,128)(2,1)} custom-call(bf16[512,512]{1,0:T(8,128)(2,1)S(1)} %fusion.15.table, bf16[512,128]{1,0:T(8,128)(2,1)S(1)} %get-tuple-element.41.proj, bf16[512,2048]{1,0:T(8,128)(2,1)S(1)} %pad_maximum_fusion.5.values.operand, bf16[3,128,2048]{2,1,0:T(8,128)(2,1)S(1)} %pad_maximum_fusion.10.states, f32[8,512,44]{2,1,0:T(8,128)S(1)} %bitcast.154, ...), custom_call_target="tpu_custom_call" | custom-call | flops 1342177280 | bytes 5242880 | tf_op jit(solution)/shard_map/forward/pallas_call | solution.py:171
  448.2 33.7 %collective-permute-done.43 = bf16[2048,512]{0,1:T(8,128)(2,1)S(1)} collective-permute-done((bf16[2048,512]{0,1:T(8,128)(2,1)}, bf16[2048,512]{0,1:T(8,128)(2,1)S(1)}, u32[]{:S(2)}, u32[]{:S(2)}) %collective-permute-start.43) | collective-permute-done | bytes 2097184 | tf_op jit(solution)/shard_map/ppermute | solution.py:20
  483.9 17.5 %collective-permute-done.35 = bf16[1024,512]{0,1:T(8,128)(2,1)S(1)} collective-permute-done((bf16[1024,512]{0,1:T(8,128)(2,1)S(1)}, bf16[1024,512]{0,1:T(8,128)(2,1)S(1)}, u32[]{:S(2)}, u32[]{:S(2)}) %collective-permute-start.35) | collective-permute-done | bytes 1048608 | tf_op jit(solution)/shard_map/ppermute | solution.py:20
  507.1 13.5 %collective-permute-done.44 = bf16[1024,512]{0,1:T(8,128)(2,1)S(1)} collective-permute-done((bf16[1024,512]{0,1:T(8,128)(2,1)S(1)}, bf16[1024,512]{0,1:T(8,128)(2,1)S(1)}, u32[]{:S(2)}, u32[]{:S(2)}) %collective-permute-start.44) | collective-permute-done | bytes 1048608 | tf_op jit(solution)/shard_map/ppermute | solution.py:20
  521.3 41.3 %collective-permute-done.36 = bf16[512,512]{0,1:T(8,128)(2,1)S(1)} collective-permute-done((bf16[512,512]{0,1:T(8,128)(2,1)S(1)}, bf16[512,512]{0,1:T(8,128)(2,1)S(1)}, u32[]{:S(2)}, u32[]{:S(2)}) %collective-permute-start.36) | collective-permute-done | bytes 524320 | tf_op jit(solution)/shard_map/ppermute | solution.py:20
  562.7 11.1 %collective-permute-done.39 = bf16[512,512]{0,1:T(8,128)(2,1)S(1)} collective-permute-done((bf16[512,512]{0,1:T(8,128)(2,1)S(1)}, bf16[512,512]{0,1:T(8,128)(2,1)S(1)}, u32[]{:S(2)}, u32[]{:S(2)}) %collective-permute-start.39) | collective-permute-done | bytes 524320 | tf_op jit(solution)/shard_map/ppermute | solution.py:20
  573.9 11.1 %collective-permute-done.42 = bf16[512,512]{0,1:T(8,128)(2,1)S(1)} collective-permute-done((bf16[512,512]{0,1:T(8,128)(2,1)S(1)}, bf16[512,512]{0,1:T(8,128)(2,1)S(1)}, u32[]{:S(2)}, u32[]{:S(2)}) %collective-permute-start.42) | collective-permute-done | bytes 524320 | tf_op jit(solution)/shard_map/ppermute | solution.py:20
  (259 shorter events, 139.0 us)
Async XLA Ops:
  7.2 124.4 %all-gather.3.cloned.1.call-start = ((), (), s32[]{:S(2)}) async-start(), calls=%async_computation | async-start | bytes 5242880 | tf_op jit(solution)/shard_map/all_gather | solution.py:191
  33.5 64.0 %collective-permute-start.31 = (bf16[3,128,2048]{2,1,0:T(8,128)(2,1)}, bf16[3,128,2048]{2,1,0:T(8,128)(2,1)}, u32[]{:S(2)}, u32[]{:S(2)}) collective-permute-start(bf16[3,128,2048]{2,1,0:T(8,128)(2,1)} %pad_maximum_fusion.11), channel_id=1, source_target_pairs={{0,4},{4,0},{8,12},{12,8},{16,20},{20,16},{24,28},{28,24},{1,5},{5... | collective-permute-start | bytes 4718600 | tf_op jit(solution)/shard_map/ppermute | solution.py:20
  36.2 98.7 %collective-permute-start = (bf16[512,512]{1,0:T(8,128)(2,1)}, bf16[512,512]{1,0:T(8,128)(2,1)}, u32[]{:S(2)}, u32[]{:S(2)}) collective-permute-start(bf16[512,512]{1,0:T(8,128)(2,1)} %get-tuple-element.29), channel_id=1, source_target_pairs={{0,16},{4,20},{8,24},{12,28},{16,0},{20,4},{24,8},{28,12},{1,17},{... | collective-permute-start | bytes 1572872 | tf_op jit(solution)/shard_map/ppermute | solution.py:20
  38.9 101.2 %collective-permute-start.1 = (bf16[512,512]{1,0:T(8,128)(2,1)}, bf16[512,512]{1,0:T(8,128)(2,1)}, u32[]{:S(2)}, u32[]{:S(2)}) collective-permute-start(bf16[512,512]{1,0:T(8,128)(2,1)} %get-tuple-element.29), channel_id=1, source_target_pairs={{0,4},{4,0},{8,12},{12,8},{16,20},{20,16},{24,28},{28,24},{1,5},{5... | collective-permute-start | bytes 1572872 | tf_op jit(solution)/shard_map/ppermute | solution.py:20
  39.9 98.0 %collective-permute-start.3 = (bf16[512,512]{1,0:T(8,128)(2,1)}, bf16[512,512]{1,0:T(8,128)(2,1)}, u32[]{:S(2)}, u32[]{:S(2)}) collective-permute-start(bf16[512,512]{1,0:T(8,128)(2,1)} %get-tuple-element.29), channel_id=1, source_target_pairs={{0,8},{4,12},{8,0},{12,4},{16,24},{20,28},{24,16},{28,20},{1,9},{5... | collective-permute-start | bytes 1572872 | tf_op jit(solution)/shard_map/ppermute | solution.py:20
  41.6 116.6 %collective-permute-start.7 = (bf16[512,512]{1,0:T(8,128)(2,1)}, bf16[512,512]{1,0:T(8,128)(2,1)}, u32[]{:S(2)}, u32[]{:S(2)}) collective-permute-start(bf16[512,512]{1,0:T(8,128)(2,1)} %get-tuple-element.30), channel_id=1, source_target_pairs={{0,16},{4,20},{8,24},{12,28},{16,0},{20,4},{24,8},{28,12},{1,17},{... | collective-permute-start | bytes 1572872 | tf_op jit(solution)/shard_map/ppermute | solution.py:20
  126.1 59.0 %collective-permute-start.8 = (bf16[512,512]{1,0:T(8,128)(2,1)}, bf16[512,512]{1,0:T(8,128)(2,1)}, u32[]{:S(2)}, u32[]{:S(2)}) collective-permute-start(bf16[512,512]{1,0:T(8,128)(2,1)} %get-tuple-element.30), channel_id=1, source_target_pairs={{0,8},{4,12},{8,0},{12,4},{16,24},{20,28},{24,16},{28,20},{1,9},{5... | collective-permute-start | bytes 1572872 | tf_op jit(solution)/shard_map/ppermute | solution.py:20
  134.9 54.3 %collective-permute-start.10 = (bf16[512,512]{1,0:T(8,128)(2,1)}, bf16[512,512]{1,0:T(8,128)(2,1)S(1)}, u32[]{:S(2)}, u32[]{:S(2)}) collective-permute-start(bf16[512,512]{1,0:T(8,128)(2,1)} %get-tuple-element.30), channel_id=1, source_target_pairs={{0,4},{4,0},{8,12},{12,8},{16,20},{20,16},{24,28},{28,24},{1,5},{5... | collective-permute-start | bytes 1572872 | tf_op jit(solution)/shard_map/ppermute | solution.py:20
  140.1 48.0 %collective-permute-start.14 = (bf16[512,512]{1,0:T(8,128)(2,1)S(1)}, bf16[512,512]{1,0:T(8,128)(2,1)S(1)}, u32[]{:S(2)}, u32[]{:S(2)}) collective-permute-start(bf16[512,512]{1,0:T(8,128)(2,1)S(1)} %copy-done.15), channel_id=1, source_target_pairs={{0,16},{4,20},{8,24},{12,28},{16,0},{20,4},{24,8},{28,12},{1,17},{... | collective-permute-start | bytes 1572872 | tf_op jit(solution)/shard_map/ppermute | solution.py:20
  172.5 45.3 %collective-permute-start.15 = (bf16[512,512]{1,0:T(8,128)(2,1)S(1)}, bf16[512,512]{1,0:T(8,128)(2,1)S(1)}, u32[]{:S(2)}, u32[]{:S(2)}) collective-permute-start(bf16[512,512]{1,0:T(8,128)(2,1)S(1)} %copy-done.15), channel_id=1, source_target_pairs={{0,8},{4,12},{8,0},{12,4},{16,24},{20,28},{24,16},{28,20},{1,9},{5... | collective-permute-start | bytes 1572872 | tf_op jit(solution)/shard_map/ppermute | solution.py:20
  246.4 56.4 %collective-permute-start.25 = (bf16[512,512]{1,0:T(8,128)(2,1)S(1)}, bf16[512,512]{1,0:T(8,128)(2,1)S(1)}, u32[]{:S(2)}, u32[]{:S(2)}) collective-permute-start(bf16[512,512]{1,0:T(8,128)(2,1)S(1)} %collective-permute-done.21), channel_id=1, source_target_pairs={{0,4},{4,0},{8,12},{12,8},{16,20},{20,16},{24,28},{28,24},{1,5},{5... | collective-permute-start | bytes 1572872 | tf_op jit(solution)/shard_map/ppermute | solution.py:20
  247.4 54.8 %collective-permute-start.26 = (bf16[512,512]{1,0:T(8,128)(2,1)S(1)}, bf16[512,512]{1,0:T(8,128)(2,1)S(1)}, u32[]{:S(2)}, u32[]{:S(2)}) collective-permute-start(bf16[512,512]{1,0:T(8,128)(2,1)S(1)} %collective-permute-done.22), channel_id=1, source_target_pairs={{0,4},{4,0},{8,12},{12,8},{16,20},{20,16},{24,28},{28,24},{1,5},{5... | collective-permute-start | bytes 1572872 | tf_op jit(solution)/shard_map/ppermute | solution.py:20
  340.4 97.6 %collective-permute-start.34 = (bf16[2048,512]{0,1:T(8,128)(2,1)S(1)}, bf16[2048,512]{0,1:T(8,128)(2,1)S(1)}, u32[]{:S(2)}, u32[]{:S(2)}) collective-permute-start(bf16[2048,512]{0,1:T(8,128)(2,1)S(1)} %convolution_convert_fusion.6), channel_id=1, source_target_pairs={{0,8},{4,12},{8,0},{12,4},{16,24},{20,28},{24,16},{28,20},{1,9},{5... | collective-permute-start | bytes 6291464 | tf_op jit(solution)/shard_map/ppermute | solution.py:20
  343.4 97.3 %collective-permute-start.37 = (bf16[2048,512]{0,1:T(8,128)(2,1)S(1)}, bf16[2048,512]{0,1:T(8,128)(2,1)S(1)}, u32[]{:S(2)}, u32[]{:S(2)}) collective-permute-start(bf16[2048,512]{0,1:T(8,128)(2,1)S(1)} %convolution_convert_fusion.4), channel_id=1, source_target_pairs={{0,4},{4,0},{8,12},{12,8},{16,20},{20,16},{24,28},{28,24},{1,5},{5... | collective-permute-start | bytes 6291464 | tf_op jit(solution)/shard_map/ppermute | solution.py:20
  359.8 45.4 %collective-permute-start.30 = (bf16[128,2048]{1,0:T(8,128)(2,1)S(1)}, bf16[128,2048]{1,0:T(8,128)(2,1)S(1)}, u32[]{:S(2)}, u32[]{:S(2)}) collective-permute-start(bf16[128,2048]{1,0:T(8,128)(2,1)S(1)} %get-tuple-element.34), channel_id=1, source_target_pairs={{0,16},{4,20},{8,24},{12,28},{16,0},{20,4},{24,8},{28,12},{1,17},{... | collective-permute-start | bytes 1572872 | tf_op jit(solution)/shard_map/ppermute | solution.py:20
  362.7 82.3 %collective-permute-start.40 = (bf16[2048,512]{0,1:T(8,128)(2,1)}, bf16[2048,512]{0,1:T(8,128)(2,1)}, u32[]{:S(2)}, u32[]{:S(2)}) collective-permute-start(bf16[2048,512]{0,1:T(8,128)(2,1)} %convolution_convert_fusion.2), channel_id=1, source_target_pairs={{0,4},{4,0},{8,12},{12,8},{16,20},{20,16},{24,28},{28,24},{1,5},{5... | collective-permute-start | bytes 6291464 | tf_op jit(solution)/shard_map/ppermute | solution.py:20
  366.2 115.7 %collective-permute-start.43 = (bf16[2048,512]{0,1:T(8,128)(2,1)}, bf16[2048,512]{0,1:T(8,128)(2,1)S(1)}, u32[]{:S(2)}, u32[]{:S(2)}) collective-permute-start(bf16[2048,512]{0,1:T(8,128)(2,1)} %convolution_convert_fusion), channel_id=1, source_target_pairs={{0,4},{4,0},{8,12},{12,8},{16,20},{20,16},{24,28},{28,24},{1,5},{5... | collective-permute-start | bytes 6291464 | tf_op jit(solution)/shard_map/ppermute | solution.py:20
  439.5 61.8 %collective-permute-start.35 = (bf16[1024,512]{0,1:T(8,128)(2,1)S(1)}, bf16[1024,512]{0,1:T(8,128)(2,1)S(1)}, u32[]{:S(2)}, u32[]{:S(2)}) collective-permute-start(bf16[1024,512]{0,1:T(8,128)(2,1)S(1)} %slice.343), channel_id=1, source_target_pairs={{0,4},{4,0},{8,12},{12,8},{16,20},{20,16},{24,28},{28,24},{1,5},{5... | collective-permute-start | bytes 3145736 | tf_op jit(solution)/shard_map/ppermute | solution.py:20
  442.1 61.0 %collective-permute-start.38 = (bf16[1024,512]{0,1:T(8,128)(2,1)S(1)}, bf16[1024,512]{0,1:T(8,128)(2,1)S(1)}, u32[]{:S(2)}, u32[]{:S(2)}) collective-permute-start(bf16[1024,512]{0,1:T(8,128)(2,1)S(1)} %slice.342), channel_id=1, source_target_pairs={{0,8},{4,12},{8,0},{12,4},{16,24},{20,28},{24,16},{28,20},{1,9},{5... | collective-permute-start | bytes 3145736 | tf_op jit(solution)/shard_map/ppermute | solution.py:20
  448.1 57.1 %collective-permute-start.41 = (bf16[1024,512]{0,1:T(8,128)(2,1)S(1)}, bf16[1024,512]{0,1:T(8,128)(2,1)S(1)}, u32[]{:S(2)}, u32[]{:S(2)}) collective-permute-start(bf16[1024,512]{0,1:T(8,128)(2,1)S(1)} %slice.341), channel_id=1, source_target_pairs={{0,8},{4,12},{8,0},{12,4},{16,24},{20,28},{24,16},{28,20},{1,9},{5... | collective-permute-start | bytes 3145736 | tf_op jit(solution)/shard_map/ppermute | solution.py:20
  501.8 60.8 %collective-permute-start.36 = (bf16[512,512]{0,1:T(8,128)(2,1)S(1)}, bf16[512,512]{0,1:T(8,128)(2,1)S(1)}, u32[]{:S(2)}, u32[]{:S(2)}) collective-permute-start(bf16[512,512]{0,1:T(8,128)(2,1)S(1)} %slice.347), channel_id=1, source_target_pairs={{0,16},{4,20},{8,24},{12,28},{16,0},{20,4},{24,8},{28,12},{1,17},{... | collective-permute-start | bytes 1572872 | tf_op jit(solution)/shard_map/ppermute | solution.py:20
  503.5 70.2 %collective-permute-start.39 = (bf16[512,512]{0,1:T(8,128)(2,1)S(1)}, bf16[512,512]{0,1:T(8,128)(2,1)S(1)}, u32[]{:S(2)}, u32[]{:S(2)}) collective-permute-start(bf16[512,512]{0,1:T(8,128)(2,1)S(1)} %slice.346), channel_id=1, source_target_pairs={{0,16},{4,20},{8,24},{12,28},{16,0},{20,4},{24,8},{28,12},{1,17},{... | collective-permute-start | bytes 1572872 | tf_op jit(solution)/shard_map/ppermute | solution.py:20
  505.7 79.3 %collective-permute-start.42 = (bf16[512,512]{0,1:T(8,128)(2,1)S(1)}, bf16[512,512]{0,1:T(8,128)(2,1)S(1)}, u32[]{:S(2)}, u32[]{:S(2)}) collective-permute-start(bf16[512,512]{0,1:T(8,128)(2,1)S(1)} %slice.345), channel_id=1, source_target_pairs={{0,16},{4,20},{8,24},{12,28},{16,0},{20,4},{24,8},{28,12},{1,17},{... | collective-permute-start | bytes 1572872 | tf_op jit(solution)/shard_map/ppermute | solution.py:20
  521.2 71.1 %collective-permute-start.45 = (bf16[512,512]{0,1:T(8,128)(2,1)S(1)}, bf16[512,512]{0,1:T(8,128)(2,1)S(1)}, u32[]{:S(2)}, u32[]{:S(2)}) collective-permute-start(bf16[512,512]{0,1:T(8,128)(2,1)S(1)} %slice.344), channel_id=1, source_target_pairs={{0,16},{4,20},{8,24},{12,28},{16,0},{20,4},{24,8},{28,12},{1,17},{... | collective-permute-start | bytes 1572872 | tf_op jit(solution)/shard_map/ppermute | solution.py:20
  (51 other events, 864.4 us)
Sparse Core Ops, SparseCore 0:
  9.6 37.1 all-gather.2

commit v3 on v2

--- a/solution.py
+++ b/solution.py
@@ -117,7 +117,7 @@
 def bit_orders(bits):
     straight = list(range(bits))
     turned = straight[1:2] + straight[:1] + straight[2:]
-    return [turned, straight, straight, straight]
+    return [turned, straight, turned, straight]
 
 
 def gathered(block, order):
@@ -127,7 +127,7 @@
     return have
 
 
-def scattered(blocks_t, grads, order):
+def scatter_terms(blocks_t, grads):
     half = blocks_t.shape[1] // 2
 
     def product(part):
@@ -135,14 +135,14 @@
             part, grads, (((0,), (0,)), ((), ())), preferred_element_type=jnp.float32
         ).astype(jnp.bfloat16)
 
-    send, keep = product(blocks_t[:, half:]), product(blocks_t[:, :half])
-    for step, bit in enumerate(order):
-        arrived = swapped(send, "seq", bit)
-        total = keep.astype(jnp.float32) + arrived.astype(jnp.float32)
-        half = total.shape[0] // 2
-        if step + 1 == len(order):
-            return total.astype(jnp.bfloat16)
-        keep, send = total[:half], total[half:].astype(jnp.bfloat16)
+    return product(blocks_t[:, half:]), product(blocks_t[:, :half])
+
+
+def scatter_step(send, keep, bit):
+    arrived = swapped(send, "seq", bit)
+    total = keep.astype(jnp.float32) + arrived.astype(jnp.float32)
+    half = total.shape[0] // 2
+    return total[half:].astype(jnp.bfloat16), total[:half], total
 
 
 def marks_of(order):
@@ -183,9 +183,6 @@
 
 
 def per_device(tokens, in_weight, write_proj, read_proj, log_decay, level_gain, out_grad):
-    orders = bit_orders(lax.axis_size("seq").bit_length() - 1)
-    chunk = in_weight.shape[1] // len(orders)
-    pieces = [gathered(in_weight[:, i * chunk : (i + 1) * chunk], order) for i, order in enumerate(orders)]
     both = lax.all_gather(jnp.concatenate([write_proj, read_proj], axis=1), "head", axis=0, tiled=True)
     write_rows, read_rows = both[:, :STATE], both[:, STATE:]
     full_tokens = lax.all_gather(tokens, "head", axis=0, tiled=True)
@@ -203,6 +200,10 @@
     cumulative = jnp.dot(log_decay, upper_ones, precision=lax.Precision.HIGHEST)
     totals = cumulative[:, -1]
     all_totals = lax.all_gather(totals, "seq", axis=0, tiled=False)
+    in_weight, all_totals = lax.optimization_barrier((in_weight, all_totals))
+    orders = bit_orders(lax.axis_size("seq").bit_length() - 1)
+    chunk = in_weight.shape[1] // len(orders)
+    pieces = [gathered(in_weight[:, i * chunk : (i + 1) * chunk], order) for i, order in enumerate(orders)]
 
     names = ["cum", "g0", "g1"]
     vectors = [cumulative, level_gain[0], level_gain[1]]
@@ -277,8 +278,14 @@
     for i, order in enumerate(orders):
         marks = marks_of(order)
         ordered = jnp.concatenate([blocks[r] for r in marks], axis=1)
-        parts.append(scattered(ordered, values_grad[:, i * chunk : (i + 1) * chunk], order))
-    weight_grad = jnp.concatenate(parts, axis=1)
+        send, keep = scatter_terms(ordered, values_grad[:, i * chunk : (i + 1) * chunk])
+        parts.append(scatter_step(send, keep, order[0]))
+    second_sends = [part[0] for part in parts]
+    for step in range(1, seq_count):
+        parts = [
+            scatter_step(part[0], part[1], order[step]) for part, order in zip(parts, orders)
+        ]
+    weight_grad = jnp.concatenate([part[2].astype(jnp.bfloat16) for part in parts], axis=1)
 
     chunks = []
     for have in pieces:
@@ -305,9 +312,10 @@
             partner_decays[bit] * block_state + partner,
         )
         prefix = jnp.where(is_upper, partner_decays[bit] * prefix, prefix)
+    values_late = lax.optimization_barrier((values, *second_sends))[0]
     layer_out = call(
         functools.partial(local_kernel, names, group, levels, False),
-        groups, width, [scores, read_rows], [values, jnp.stack(buckets)], [cols, rows],
+        groups, width, [scores, read_rows], [values_late, jnp.stack(buckets)], [cols, rows],
         jax.ShapeDtypeStruct((tok_len, columns), jnp.bfloat16), local_work, "forward",
     )
     return (layer_out, weight_grad)

time: 607 us -> 609 us (level)
  local copies, waits for them, and re-layouts: 21 us -> 27.4 us
    unnamed x64 -> x70, local copies, waits for them, and re-layouts: 11.6 us -> 13.1 us
  transfers between devices with their start and end apart: 47 -> 47, of which waited for: 22 -> 20; matrix products, arithmetic and copies ran while one was open for 10% -> 11% of each run, Pallas kernels for 11% -> 11%
where the time goes in v3:
time: 609 us; the launch traced here: 599 us
  waiting for transfers between devices  340 us (56%)
  Pallas kernels  64.9 us (11%)
  blocking collectives  55.7 us (9%)
  starting transfers between devices  46.9 us (8%)
  matrix products  31.3 us (5%)
  local copies, waits for them, and re-layouts  27.4 us (4%)
  between operations  16.3 us (3%)
  other arithmetic  16.1 us (3%)
    ppermute x46, waiting for transfers between devices, swapped(): return lax.ppermute(value, axis, pairs)  340 us
    pallas_call x4, Pallas kernels, call(): pl.pallas_call(kernel, grid=(groups,), in_specs=[whole_spec(a) for a in f...  64.9 us
    unnamed x1, blocking collectives  48.5 us
    ppermute x46, starting transfers between devices, swapped(): return lax.ppermute(value, axis, pairs)  46.8 us
    dot_general x34, matrix products, dot32(): return jnp.dot(left, right, preferred_element_type=jnp.float32)  20.6 us
    unnamed x70, local copies, waits for them, and re-layouts  13.1 us
  transfers between devices with their start and end apart: 47, of which 20 were waited for; matrix products, arithmetic and copies ran while one was open for 11% of the time, Pallas kernels for 11%

profile of v3, /device:TPU:0, one launch (start us, length us, event | category | flops | bytes accessed | tf_op | source)
XLA Modules:
  0.0 599.1 jit_solution(11450569039444225612)
XLA Ops:
  12.5 7.2 %all_gather.9 = bf16[512,256]{1,0:T(8,128)(2,1)S(1)} all-gather(bf16[128,256]{1,0:T(8,128)(2,1)S(1)} %pad_maximum_fusion.21), channel_id=1, replica_groups=mesh['seq'=8,'head'=4] {'head'}, dimensions={0}, use_global_device_ids=true | all-gather | bytes 327680 | tf_op jit(solution)/shard_map/all_gather | solution.py:186
  21.9 9.4 %level_grads.1 = f32[3,128,2048]{2,1,0:T(8,128)S(1)} custom-call(bf16[128,512]{1,0:T(8,128)(2,1)S(1)} %copy.131.read_t, bf16[512,2048]{1,0:T(8,128)(2,1)S(1)} %copy-done.4, f32[8,512,44]{2,1,0:T(8,128)S(1)} %bitcast.151), custom_call_target="tpu_custom_call" | custom-call | flops 805306368 | bytes 2949120 | tf_op jit(solution)/shard_map/level_grads/pallas_call | solution.py:171
  36.4 48.5 %all-reduce = f32[256]{0:T(256)S(1)} all-reduce(f32[256]{0:T(256)S(1)} %dynamic-update-slice), channel_id=2, replica_groups=mesh['seq'=8,'head'=4] {'seq'}, use_global_device_ids=true, to_apply=%add | all-reduce | flops 256 | bytes 2048
  102.6 42.0 %collective-permute-done.29 = bf16[2,128,2048]{2,1,0:T(8,128)(2,1)} collective-permute-done((bf16[2,128,2048]{2,1,0:T(8,128)(2,1)}, bf16[2,128,2048]{2,1,0:T(8,128)(2,1)}, u32[]{:S(2)}, u32[]{:S(2)}) %collective-permute-start.29) | collective-permute-done | bytes 1048608 | tf_op jit(solution)/shard_map/ppermute | solution.py:20
  163.1 11.7 %collective-permute-done.2 = bf16[512,512]{1,0:T(8,128)(2,1)S(1)} collective-permute-done((bf16[512,512]{1,0:T(8,128)(2,1)}, bf16[512,512]{1,0:T(8,128)(2,1)S(1)}, u32[]{:S(2)}, u32[]{:S(2)}) %collective-permute-start.2) | collective-permute-done | bytes 524320 | tf_op jit(solution)/shard_map/ppermute | solution.py:20
  179.3 12.2 %collective-permute-done.5 = bf16[512,512]{1,0:T(8,128)(2,1)S(1)} collective-permute-done((bf16[512,512]{1,0:T(8,128)(2,1)}, bf16[512,512]{1,0:T(8,128)(2,1)S(1)}, u32[]{:S(2)}, u32[]{:S(2)}) %collective-permute-start.5) | collective-permute-done | bytes 524320 | tf_op jit(solution)/shard_map/ppermute | solution.py:20
  193.2 9.4 %collective-permute-done.4 = bf16[512,512]{1,0:T(8,128)(2,1)S(1)} collective-permute-done((bf16[512,512]{1,0:T(8,128)(2,1)}, bf16[512,512]{1,0:T(8,128)(2,1)S(1)}, u32[]{:S(2)}, u32[]{:S(2)}) %collective-permute-start.4) | collective-permute-done | bytes 524320 | tf_op jit(solution)/shard_map/ppermute | solution.py:20
  210.8 10.8 %collective-permute-done.12 = bf16[512,512]{1,0:T(8,128)(2,1)S(1)} collective-permute-done((bf16[512,512]{1,0:T(8,128)(2,1)}, bf16[512,512]{1,0:T(8,128)(2,1)S(1)}, u32[]{:S(2)}, u32[]{:S(2)}) %collective-permute-start.12) | collective-permute-done | bytes 524320 | tf_op jit(solution)/shard_map/ppermute | solution.py:20
  223.8 15.1 %collective-permute-done.9 = bf16[512,512]{1,0:T(8,128)(2,1)S(1)} collective-permute-done((bf16[512,512]{1,0:T(8,128)(2,1)}, bf16[512,512]{1,0:T(8,128)(2,1)S(1)}, u32[]{:S(2)}, u32[]{:S(2)}) %collective-permute-start.9) | collective-permute-done | bytes 524320 | tf_op jit(solution)/shard_map/ppermute | solution.py:20
  245.7 19.3 %collective-permute-done.19 = bf16[512,512]{1,0:T(8,128)(2,1)S(1)} collective-permute-done((bf16[512,512]{1,0:T(8,128)(2,1)S(1)}, bf16[512,512]{1,0:T(8,128)(2,1)S(1)}, u32[]{:S(2)}, u32[]{:S(2)}) %collective-permute-start.19) | collective-permute-done | bytes 524320 | tf_op jit(solution)/shard_map/ppermute | solution.py:20
  268.3 7.9 %collective-permute-done.18 = bf16[512,512]{1,0:T(8,128)(2,1)S(1)} collective-permute-done((bf16[512,512]{1,0:T(8,128)(2,1)S(1)}, bf16[512,512]{1,0:T(8,128)(2,1)S(1)}, u32[]{:S(2)}, u32[]{:S(2)}) %collective-permute-start.18) | collective-permute-done | bytes 524320 | tf_op jit(solution)/shard_map/ppermute | solution.py:20
  279.6 7.9 %collective-permute-done.23 = bf16[512,512]{1,0:T(8,128)(2,1)S(1)} collective-permute-done((bf16[512,512]{1,0:T(8,128)(2,1)S(1)}, bf16[512,512]{1,0:T(8,128)(2,1)S(1)}, u32[]{:S(2)}, u32[]{:S(2)}) %collective-permute-start.23) | collective-permute-done | bytes 524320 | tf_op jit(solution)/shard_map/ppermute | solution.py:20
  288.3 10.5 %collective-permute-done.6 = bf16[512,512]{1,0:T(8,128)(2,1)S(1)} collective-permute-done((bf16[512,512]{1,0:T(8,128)(2,1)S(1)}, bf16[512,512]{1,0:T(8,128)(2,1)S(1)}, u32[]{:S(2)}, u32[]{:S(2)}) %collective-permute-start.6) | collective-permute-done | bytes 524320 | tf_op jit(solution)/shard_map/ppermute | solution.py:20
  302.4 14.3 %collective-permute-done.20 = bf16[512,512]{1,0:T(8,128)(2,1)S(1)} collective-permute-done((bf16[512,512]{1,0:T(8,128)(2,1)S(1)}, bf16[512,512]{1,0:T(8,128)(2,1)S(1)}, u32[]{:S(2)}, u32[]{:S(2)}) %collective-permute-start.20) | collective-permute-done | bytes 524320 | tf_op jit(solution)/shard_map/ppermute | solution.py:20
  318.8 4.9 seg_state.1
  327.3 18.4 %backward.1 = bf16[512,2048]{1,0:T(8,128)(2,1)S(1)} custom-call(bf16[512,512]{1,0:T(8,128)(2,1)S(1)} %copy-done.6, bf16[512,128]{1,0:T(8,128)(2,1)S(1)} %get-tuple-element.46.proj, bf16[512,2048]{1,0:T(8,128)(2,1)S(1)} %copy-done.5, bf16[128,2048]{1,0:T(8,128)(2,1)S(1)} %fusion.30.states, f32[8,512,44]{2,1,0:T(8,128)S(1)} %bitcast.153, ...), custom_call_target="tpu_custom_call" | custom-call | flops 1342177280 | bytes 4194304 | tf_op jit(solution)/shard_map/backward/pallas_call | solution.py:171
  351.1 15.4 %collective-permute-done.36 = bf16[128,2048]{1,0:T(8,128)(2,1)S(1)} collective-permute-done((bf16[128,2048]{1,0:T(8,128)(2,1)S(1)}, bf16[128,2048]{1,0:T(8,128)(2,1)S(1)}, u32[]{:S(2)}, u32[]{:S(2)}) %collective-permute-start.36) | collective-permute-done | bytes 524320 | tf_op jit(solution)/shard_map/ppermute | solution.py:20
  372.5 42.0 %collective-permute-done.37 = bf16[128,2048]{1,0:T(8,128)(2,1)S(1)} collective-permute-done((bf16[128,2048]{1,0:T(8,128)(2,1)S(1)}, bf16[128,2048]{1,0:T(8,128)(2,1)S(1)}, u32[]{:S(2)}, u32[]{:S(2)}) %collective-permute-start.37) | collective-permute-done | bytes 524320 | tf_op jit(solution)/shard_map/ppermute | solution.py:20
  423.1 38.8 %collective-permute-done.33 = bf16[2048,512]{0,1:T(8,128)(2,1)S(1)} collective-permute-done((bf16[2048,512]{0,1:T(8,128)(2,1)S(1)}, bf16[2048,512]{0,1:T(8,128)(2,1)S(1)}, u32[]{:S(2)}, u32[]{:S(2)}) %collective-permute-start.33) | collective-permute-done | bytes 2097184 | tf_op jit(solution)/shard_map/ppermute | solution.py:20
  468.6 32.3 %forward.1 = bf16[512,2048]{1,0:T(8,128)(2,1)} custom-call(bf16[512,512]{1,0:T(8,128)(2,1)S(1)} %fusion.8.table, bf16[512,128]{1,0:T(8,128)(2,1)S(1)} %get-tuple-element.47.proj, bf16[512,2048]{1,0:T(8,128)(2,1)S(1)} %pad_maximum_fusion.4.values.operand, bf16[3,128,2048]{2,1,0:T(8,128)(2,1)S(1)} %pad_maximum_fusion.10.states, f32[8,512,44]{2,1,0:T(8,128)S(1)} %bitcast.154, ...), custom_call_target="tpu_custom_call" | custom-call | flops 1342177280 | bytes 5242880 | tf_op jit(solution)/shard_map/forward/pallas_call | solution.py:171
  509.3 50.6 %collective-permute-done.39 = bf16[512,512]{0,1:T(8,128)(2,1)S(1)} collective-permute-done((bf16[512,512]{0,1:T(8,128)(2,1)S(1)}, bf16[512,512]{0,1:T(8,128)(2,1)S(1)}, u32[]{:S(2)}, u32[]{:S(2)}) %collective-permute-start.39) | collective-permute-done | bytes 524320 | tf_op jit(solution)/shard_map/ppermute | solution.py:20
  560.0 11.1 %collective-permute-done.41 = bf16[512,512]{0,1:T(8,128)(2,1)S(1)} collective-permute-done((bf16[512,512]{0,1:T(8,128)(2,1)S(1)}, bf16[512,512]{0,1:T(8,128)(2,1)S(1)}, u32[]{:S(2)}, u32[]{:S(2)}) %collective-permute-start.41) | collective-permute-done | bytes 524320 | tf_op jit(solution)/shard_map/ppermute | solution.py:20
  571.2 11.1 %collective-permute-done.43 = bf16[512,512]{0,1:T(8,128)(2,1)S(1)} collective-permute-done((bf16[512,512]{0,1:T(8,128)(2,1)S(1)}, bf16[512,512]{0,1:T(8,128)(2,1)S(1)}, u32[]{:S(2)}, u32[]{:S(2)}) %collective-permute-start.43) | collective-permute-done | bytes 524320 | tf_op jit(solution)/shard_map/ppermute | solution.py:20
  582.5 6.6 %collective-permute-done.45 = bf16[512,512]{0,1:T(8,128)(2,1)S(1)} collective-permute-done((bf16[512,512]{0,1:T(8,128)(2,1)S(1)}, bf16[512,512]{0,1:T(8,128)(2,1)S(1)}, u32[]{:S(2)}, u32[]{:S(2)}) %collective-permute-start.45) | collective-permute-done | bytes 524320 | tf_op jit(solution)/shard_map/ppermute | solution.py:20
  (265 shorter events, 125.6 us)
Async XLA Ops:
  7.2 143.3 %all-gather.3.cloned.1.call-start = ((), (), s32[]{:S(2)}) async-start(), calls=%async_computation | async-start | bytes 5242880 | tf_op jit(solution)/shard_map/all_gather | solution.py:188
  33.5 58.6 %collective-permute-start.28 = (bf16[3,128,2048]{2,1,0:T(8,128)(2,1)}, bf16[3,128,2048]{2,1,0:T(8,128)(2,1)}, u32[]{:S(2)}, u32[]{:S(2)}) collective-permute-start(bf16[3,128,2048]{2,1,0:T(8,128)(2,1)} %pad_maximum_fusion.9), channel_id=1, source_target_pairs={{0,4},{4,0},{8,12},{12,8},{16,20},{20,16},{24,28},{28,24},{1,5},{5... | collective-permute-start | bytes 4718600 | tf_op jit(solution)/shard_map/ppermute | solution.py:20
  87.9 65.9 %collective-permute-start = (bf16[512,512]{1,0:T(8,128)(2,1)}, bf16[512,512]{1,0:T(8,128)(2,1)}, u32[]{:S(2)}, u32[]{:S(2)}) collective-permute-start(bf16[512,512]{1,0:T(8,128)(2,1)} %get-tuple-element.35), channel_id=1, source_target_pairs={{0,16},{4,20},{8,24},{12,28},{16,0},{20,4},{24,8},{28,12},{1,17},{... | collective-permute-start | bytes 1572872 | tf_op jit(solution)/shard_map/ppermute | solution.py:20
  87.9 71.1 %collective-permute-start.1 = (bf16[512,512]{1,0:T(8,128)(2,1)}, bf16[512,512]{1,0:T(8,128)(2,1)}, u32[]{:S(2)}, u32[]{:S(2)}) collective-permute-start(bf16[512,512]{1,0:T(8,128)(2,1)} %get-tuple-element.35), channel_id=1, source_target_pairs={{0,4},{4,0},{8,12},{12,8},{16,20},{20,16},{24,28},{28,24},{1,5},{5... | collective-permute-start | bytes 1572872 | tf_op jit(solution)/shard_map/ppermute | solution.py:20
  87.9 69.4 %collective-permute-start.3 = (bf16[512,512]{1,0:T(8,128)(2,1)}, bf16[512,512]{1,0:T(8,128)(2,1)}, u32[]{:S(2)}, u32[]{:S(2)}) collective-permute-start(bf16[512,512]{1,0:T(8,128)(2,1)} %get-tuple-element.35), channel_id=1, source_target_pairs={{0,8},{4,12},{8,0},{12,4},{16,24},{20,28},{24,16},{28,20},{1,9},{5... | collective-permute-start | bytes 1572872 | tf_op jit(solution)/shard_map/ppermute | solution.py:20
  88.7 88.7 %collective-permute-start.7 = (bf16[512,512]{1,0:T(8,128)(2,1)}, bf16[512,512]{1,0:T(8,128)(2,1)}, u32[]{:S(2)}, u32[]{:S(2)}) collective-permute-start(bf16[512,512]{1,0:T(8,128)(2,1)} %get-tuple-element.38), channel_id=1, source_target_pairs={{0,16},{4,20},{8,24},{12,28},{16,0},{20,4},{24,8},{28,12},{1,17},{... | collective-permute-start | bytes 1572872 | tf_op jit(solution)/shard_map/ppermute | solution.py:20
  97.2 47.4 %collective-permute-start.29 = (bf16[2,128,2048]{2,1,0:T(8,128)(2,1)}, bf16[2,128,2048]{2,1,0:T(8,128)(2,1)}, u32[]{:S(2)}, u32[]{:S(2)}) collective-permute-start(bf16[2,128,2048]{2,1,0:T(8,128)(2,1)} %pad_maximum_fusion.11), channel_id=1, source_target_pairs={{0,8},{4,12},{8,0},{12,4},{16,24},{20,28},{24,16},{28,20},{1,9},{5... | collective-permute-start | bytes 3145736 | tf_op jit(solution)/shard_map/ppermute | solution.py:20
  144.6 58.4 %collective-permute-start.8 = (bf16[512,512]{1,0:T(8,128)(2,1)}, bf16[512,512]{1,0:T(8,128)(2,1)}, u32[]{:S(2)}, u32[]{:S(2)}) collective-permute-start(bf16[512,512]{1,0:T(8,128)(2,1)} %get-tuple-element.38), channel_id=1, source_target_pairs={{0,8},{4,12},{8,0},{12,4},{16,24},{20,28},{24,16},{28,20},{1,9},{5... | collective-permute-start | bytes 1572872 | tf_op jit(solution)/shard_map/ppermute | solution.py:20
  153.8 56.5 %collective-permute-start.10 = (bf16[512,512]{1,0:T(8,128)(2,1)}, bf16[512,512]{1,0:T(8,128)(2,1)S(1)}, u32[]{:S(2)}, u32[]{:S(2)}) collective-permute-start(bf16[512,512]{1,0:T(8,128)(2,1)} %get-tuple-element.38), channel_id=1, source_target_pairs={{0,4},{4,0},{8,12},{12,8},{16,20},{20,16},{24,28},{28,24},{1,5},{5... | collective-permute-start | bytes 1572872 | tf_op jit(solution)/shard_map/ppermute | solution.py:20
  159.0 49.1 %collective-permute-start.14 = (bf16[512,512]{1,0:T(8,128)(2,1)S(1)}, bf16[512,512]{1,0:T(8,128)(2,1)S(1)}, u32[]{:S(2)}, u32[]{:S(2)}) collective-permute-start(bf16[512,512]{1,0:T(8,128)(2,1)S(1)} %copy-done.18), channel_id=1, source_target_pairs={{0,16},{4,20},{8,24},{12,28},{16,0},{20,4},{24,8},{28,12},{1,17},{... | collective-permute-start | bytes 1572872 | tf_op jit(solution)/shard_map/ppermute | solution.py:20
  191.5 48.2 %collective-permute-start.15 = (bf16[512,512]{1,0:T(8,128)(2,1)S(1)}, bf16[512,512]{1,0:T(8,128)(2,1)S(1)}, u32[]{:S(2)}, u32[]{:S(2)}) collective-permute-start(bf16[512,512]{1,0:T(8,128)(2,1)S(1)} %copy-done.18), channel_id=1, source_target_pairs={{0,4},{4,0},{8,12},{12,8},{16,20},{20,16},{24,28},{28,24},{1,5},{5... | collective-permute-start | bytes 1572872 | tf_op jit(solution)/shard_map/ppermute | solution.py:20
  265.8 51.8 %collective-permute-start.25 = (bf16[512,512]{1,0:T(8,128)(2,1)S(1)}, bf16[512,512]{1,0:T(8,128)(2,1)S(1)}, u32[]{:S(2)}, u32[]{:S(2)}) collective-permute-start(bf16[512,512]{1,0:T(8,128)(2,1)S(1)} %collective-permute-done.21), channel_id=1, source_target_pairs={{0,4},{4,0},{8,12},{12,8},{16,20},{20,16},{24,28},{28,24},{1,5},{5... | collective-permute-start | bytes 1572872 | tf_op jit(solution)/shard_map/ppermute | solution.py:20
  267.0 50.1 %collective-permute-start.26 = (bf16[512,512]{1,0:T(8,128)(2,1)S(1)}, bf16[512,512]{1,0:T(8,128)(2,1)S(1)}, u32[]{:S(2)}, u32[]{:S(2)}) collective-permute-start(bf16[512,512]{1,0:T(8,128)(2,1)S(1)} %collective-permute-done.22), channel_id=1, source_target_pairs={{0,4},{4,0},{8,12},{12,8},{16,20},{20,16},{24,28},{28,24},{1,5},{5... | collective-permute-start | bytes 1572872 | tf_op jit(solution)/shard_map/ppermute | solution.py:20
  347.3 69.7 %collective-permute-start.31 = (bf16[2048,512]{0,1:T(8,128)(2,1)S(1)}, bf16[2048,512]{0,1:T(8,128)(2,1)S(1)}, u32[]{:S(2)}, u32[]{:S(2)}) collective-permute-start(bf16[2048,512]{0,1:T(8,128)(2,1)S(1)} %convolution_convert_fusion.6), channel_id=1, source_target_pairs={{0,8},{4,12},{8,0},{12,4},{16,24},{20,28},{24,16},{28,20},{1,9},{5... | collective-permute-start | bytes 6291464 | tf_op jit(solution)/shard_map/ppermute | solution.py:20
  350.7 69.3 %collective-permute-start.32 = (bf16[2048,512]{0,1:T(8,128)(2,1)S(1)}, bf16[2048,512]{0,1:T(8,128)(2,1)S(1)}, u32[]{:S(2)}, u32[]{:S(2)}) collective-permute-start(bf16[2048,512]{0,1:T(8,128)(2,1)S(1)} %convolution_convert_fusion.4), channel_id=1, source_target_pairs={{0,4},{4,0},{8,12},{12,8},{16,20},{20,16},{24,28},{28,24},{1,5},{5... | collective-permute-start | bytes 6291464 | tf_op jit(solution)/shard_map/ppermute | solution.py:20
  367.0 47.5 %collective-permute-start.37 = (bf16[128,2048]{1,0:T(8,128)(2,1)S(1)}, bf16[128,2048]{1,0:T(8,128)(2,1)S(1)}, u32[]{:S(2)}, u32[]{:S(2)}) collective-permute-start(bf16[128,2048]{1,0:T(8,128)(2,1)S(1)} %get-tuple-element.40), channel_id=1, source_target_pairs={{0,16},{4,20},{8,24},{12,28},{16,0},{20,4},{24,8},{28,12},{1,17},{... | collective-permute-start | bytes 1572872 | tf_op jit(solution)/shard_map/ppermute | solution.py:20
  368.4 93.5 %collective-permute-start.33 = (bf16[2048,512]{0,1:T(8,128)(2,1)S(1)}, bf16[2048,512]{0,1:T(8,128)(2,1)S(1)}, u32[]{:S(2)}, u32[]{:S(2)}) collective-permute-start(bf16[2048,512]{0,1:T(8,128)(2,1)S(1)} %convolution_convert_fusion.2), channel_id=1, source_target_pairs={{0,8},{4,12},{8,0},{12,4},{16,24},{20,28},{24,16},{28,20},{1,9},{5... | collective-permute-start | bytes 6291464 | tf_op jit(solution)/shard_map/ppermute | solution.py:20
  372.2 92.6 %collective-permute-start.34 = (bf16[2048,512]{0,1:T(8,128)(2,1)S(1)}, bf16[2048,512]{0,1:T(8,128)(2,1)S(1)}, u32[]{:S(2)}, u32[]{:S(2)}) collective-permute-start(bf16[2048,512]{0,1:T(8,128)(2,1)S(1)} %convolution_convert_fusion), channel_id=1, source_target_pairs={{0,4},{4,0},{8,12},{12,8},{16,20},{20,16},{24,28},{28,24},{1,5},{5... | collective-permute-start | bytes 6291464 | tf_op jit(solution)/shard_map/ppermute | solution.py:20
  419.6 81.3 %collective-permute-start.38 = (bf16[1024,512]{0,1:T(8,128)(2,1)}, bf16[1024,512]{0,1:T(8,128)(2,1)S(1)}, u32[]{:S(2)}, u32[]{:S(2)}) collective-permute-start(bf16[1024,512]{0,1:T(8,128)(2,1)} %slice.343), channel_id=1, source_target_pairs={{0,4},{4,0},{8,12},{12,8},{16,20},{20,16},{24,28},{28,24},{1,5},{5... | collective-permute-start | bytes 3145736 | tf_op jit(solution)/shard_map/ppermute | solution.py:20
  422.5 81.3 %collective-permute-start.40 = (bf16[1024,512]{0,1:T(8,128)(2,1)}, bf16[1024,512]{0,1:T(8,128)(2,1)S(1)}, u32[]{:S(2)}, u32[]{:S(2)}) collective-permute-start(bf16[1024,512]{0,1:T(8,128)(2,1)} %slice.342), channel_id=1, source_target_pairs={{0,8},{4,12},{8,0},{12,4},{16,24},{20,28},{24,16},{28,20},{1,9},{5... | collective-permute-start | bytes 3145736 | tf_op jit(solution)/shard_map/ppermute | solution.py:20
  501.4 58.4 %collective-permute-start.39 = (bf16[512,512]{0,1:T(8,128)(2,1)S(1)}, bf16[512,512]{0,1:T(8,128)(2,1)S(1)}, u32[]{:S(2)}, u32[]{:S(2)}) collective-permute-start(bf16[512,512]{0,1:T(8,128)(2,1)S(1)} %slice.347), channel_id=1, source_target_pairs={{0,16},{4,20},{8,24},{12,28},{16,0},{20,4},{24,8},{28,12},{1,17},{... | collective-permute-start | bytes 1572872 | tf_op jit(solution)/shard_map/ppermute | solution.py:20
  504.2 66.8 %collective-permute-start.41 = (bf16[512,512]{0,1:T(8,128)(2,1)S(1)}, bf16[512,512]{0,1:T(8,128)(2,1)S(1)}, u32[]{:S(2)}, u32[]{:S(2)}) collective-permute-start(bf16[512,512]{0,1:T(8,128)(2,1)S(1)} %slice.346), channel_id=1, source_target_pairs={{0,16},{4,20},{8,24},{12,28},{16,0},{20,4},{24,8},{28,12},{1,17},{... | collective-permute-start | bytes 1572872 | tf_op jit(solution)/shard_map/ppermute | solution.py:20
  505.3 77.0 %collective-permute-start.43 = (bf16[512,512]{0,1:T(8,128)(2,1)S(1)}, bf16[512,512]{0,1:T(8,128)(2,1)S(1)}, u32[]{:S(2)}, u32[]{:S(2)}) collective-permute-start(bf16[512,512]{0,1:T(8,128)(2,1)S(1)} %slice.345), channel_id=1, source_target_pairs={{0,16},{4,20},{8,24},{12,28},{16,0},{20,4},{24,8},{28,12},{1,17},{... | collective-permute-start | bytes 1572872 | tf_op jit(solution)/shard_map/ppermute | solution.py:20
  509.2 79.9 %collective-permute-start.45 = (bf16[512,512]{0,1:T(8,128)(2,1)S(1)}, bf16[512,512]{0,1:T(8,128)(2,1)S(1)}, u32[]{:S(2)}, u32[]{:S(2)}) collective-permute-start(bf16[512,512]{0,1:T(8,128)(2,1)S(1)} %slice.344), channel_id=1, source_target_pairs={{0,16},{4,20},{8,24},{12,28},{16,0},{20,4},{24,8},{28,12},{1,17},{... | collective-permute-start | bytes 1572872 | tf_op jit(solution)/shard_map/ppermute | solution.py:20
  (54 other events, 924.8 us)
Sparse Core Ops, SparseCore 0:
  9.6 37.1 all-gather.2
